TPU v7x, 512 devices: a whole 4x4x16 slice. The times are simulated.
512 devices in a mesh: ax: 32 (over y, z_lo), circ: 8 (over z_hi, x), rad: 2 (over core).
Axes of the slice: x: 4, y: 4, z: 16 (z_hi: 2, z_lo: 8; z = z_hi * 8 + z_lo), core: 2. Of those that a mesh axis runs over, the one named last changes fastest.
Arguments:
- adjoint_rhs: bfloat16 [64, 48, 128, 256], P('ax', 'circ', None, 'rad'), may hold values from -6 to 6
- pivot_inverse: bfloat16 [64, 48, 256, 256], P('ax', 'circ', None, 'rad'), may hold values from -1 to 2
- diagonal_block: bfloat16 [64, 48, 256, 256], P('ax', 'circ', None, 'rad'), may hold values from -1 to 2
- coupling: bfloat16 [64, 48, 2, 4, 128, 128], P('ax', 'circ', 'rad'), may hold values from -0.21875 to 0.21875
- pattern: int32 [64, 48, 2, 4], P('ax', 'circ', 'rad'), may hold values 0 or 1
- wave_level: int32 [64, 48], P('ax', 'circ'), may hold values from 0 to 3, as said below
Outputs:
- first_vector: bfloat16 [64, 48, 128, 256], P('ax', 'circ', None, 'rad')
- second_vector: bfloat16 [64, 48, 128, 256], P('ax', 'circ', None, 'rad')
Inputs may be any that keep to these rules, and one draw needn't show every extreme that they name: `wave_level`: in each aligned block of 2 x 6 tiles (the tiles of one index of ax and circ) every level holds exactly 3 tiles, and tiles that share a side, around the circumference too, have levels of different parity.
All inputs are finite; a program needn't handle non-finite values. No bound on the sum of `pattern` on one device may be relied on, other than what follows from the above.
Results may differ from a plain program's by a relative error of at most 0.017.
Values may be sent and summed in bfloat16 or wider, within the bound.
A program may use at most 64 MiB of HBM per device.

v0:
```python
import jax
import jax.numpy as jnp
from jax import lax
from jax.sharding import PartitionSpec as P

NLEV = 4


def with_halo(block, sides, width, periodic):
    for axis, dim in sides:
        count = lax.axis_size(axis)
        forward = [(i, i + 1) for i in range(count - 1)]
        if periodic:
            forward.append((count - 1, 0))
        backward = [(target, source) for source, target in forward]
        low = lax.ppermute(
            lax.slice_in_dim(block, block.shape[dim] - width, None, axis=dim), axis, forward
        )
        high = lax.ppermute(lax.slice_in_dim(block, 0, width, axis=dim), axis, backward)
        block = jnp.concatenate([low, block, high], axis=dim)
    return block


def per_device(adjoint_rhs, pivot_inverse, diagonal_block, coupling, pattern, wave_level):
    tiles_axial, tiles_circ, rhs_count, cell_count = adjoint_rhs.shape
    tile_count = tiles_axial * tiles_circ
    per_level = tile_count // NLEV
    keys = wave_level.reshape(-1) * tile_count + jnp.arange(tile_count, dtype=jnp.int32)
    ordering = jnp.argsort(keys)
    chosen_list = [
        ordering[section_index * per_level : (section_index + 1) * per_level]
        for section_index in range(NLEV)
    ]
    rhs_flat = adjoint_rhs.reshape(tile_count, rhs_count, cell_count)
    pivots = pivot_inverse.reshape(tile_count, pivot_inverse.shape[2], cell_count)
    diagonals = diagonal_block.reshape(tile_count, diagonal_block.shape[2], cell_count)
    weights = coupling.reshape(tile_count, 4, cell_count, cell_count)
    present = pattern.reshape(tile_count, 4).astype(jnp.bfloat16)

    def neighbours_whole(values):
        tile_grid = values.reshape(tiles_axial, tiles_circ, rhs_count, cell_count)
        axial_pad = with_halo(tile_grid, (("ax", 0),), 1, False)
        circ_pad = with_halo(tile_grid, (("circ", 1),), 1, True)
        lower_axial = axial_pad[:-2]
        upper_axial = axial_pad[2:]
        lower_circ = circ_pad[:, :-2]
        upper_circ = circ_pad[:, 2:]
        stacked = jnp.stack([lower_axial, upper_axial, lower_circ, upper_circ], axis=2)
        return stacked.reshape(tile_count, 4, rhs_count, cell_count)

    def neighbours_sweep(values):
        return neighbours_whole(values)

    def couple(beside, present_rows, weight_rows):
        masked = beside * present_rows[:, :, None, None]
        return jnp.einsum("tdkx,tdxc->tkc", masked, weight_rows, preferred_element_type=jnp.float32)

    def pivot_apply(carried, chosen):
        whole_tile = lax.all_gather(carried, "rad", axis=2, tiled=True)
        return jnp.einsum(
            "tkx,txc->tkc", whole_tile, pivots[chosen], preferred_element_type=jnp.float32
        )

    def apply_inverse(source):
        forward = jnp.zeros((tile_count, rhs_count, cell_count), jnp.bfloat16)
        for section_index in range(NLEV):
            chosen = chosen_list[section_index]
            carried = source[chosen].astype(jnp.float32)
            if section_index > 0:
                beside = neighbours_sweep(forward)[chosen]
                carried = carried - couple(beside, present[chosen], weights[chosen])
            updated = pivot_apply(carried.astype(jnp.bfloat16), chosen).astype(jnp.bfloat16)
            forward = forward.at[chosen].set(updated)
        backward = jnp.zeros((tile_count, rhs_count, cell_count), jnp.bfloat16)
        for section_index in reversed(range(NLEV)):
            chosen = chosen_list[section_index]
            updated = forward[chosen].astype(jnp.float32)
            if section_index < NLEV - 1:
                beside = neighbours_sweep(backward)[chosen]
                carried = couple(beside, present[chosen], weights[chosen]).astype(jnp.bfloat16)
                updated = updated - pivot_apply(carried, chosen)
            backward = backward.at[chosen].set(updated.astype(jnp.bfloat16))
        return backward

    first_vector = apply_inverse(rhs_flat)
    whole_first = lax.all_gather(first_vector, "rad", axis=2, tiled=True)
    own_part = jnp.einsum(
        "tkx,txc->tkc", whole_first, diagonals, preferred_element_type=jnp.float32
    )
    operator_image = (own_part + couple(neighbours_whole(first_vector), present, weights)).astype(
        jnp.bfloat16
    )
    second_vector = apply_inverse(operator_image)
    out_shape = (tiles_axial, tiles_circ, rhs_count, cell_count)
    return (first_vector.reshape(out_shape), second_vector.reshape(out_shape))


def solution(mesh):
    return jax.shard_map(
        per_device,
        mesh=mesh,
        in_specs=(
            P("ax", "circ", None, "rad"),
            P("ax", "circ", None, "rad"),
            P("ax", "circ", None, "rad"),
            P("ax", "circ", "rad", None, None, None),
            P("ax", "circ", "rad", None),
            P("ax", "circ"),
        ),
        out_specs=(P("ax", "circ", None, "rad"), P("ax", "circ", None, "rad")),
        check_vma=False,
    )
```

profile of v0, /device:TPU:31, one launch (start us, length us, event | category | flops | bytes accessed | tf_op | source)
XLA Modules:
  0.0 584.8 jit_solution(1864478514013764626)
XLA Ops:
  14.3 11.4 %collective-permute-start.1 = (bf16[1,6,128,128]{3,2,1,0:T(8,128)(2,1)}, bf16[1,6,128,128]{3,2,1,0:T(8,128)(2,1)S(1)}, u32[]{:S(2)}, u32[]{:S(2)}) collective-permute-start(bf16[1,6,128,128]{3,2,1,0:T(8,128)(2,1)} %get-tuple-element.105), channel_id=1, source_target_pairs={{16,0},{32,16},{48,32},{64,48},{80,64},{96,80},{112,96},{128,112},... | collective-permute-start | bytes 589832 | tf_op jit(solution)/shard_map/ppermute | solution.py:19
  26.4 13.2 %collective-permute-start.2 = (bf16[2,1,128,128]{3,2,1,0:T(8,128)(2,1)}, bf16[2,1,128,128]{3,2,1,0:T(8,128)(2,1)}, u32[]{:S(2)}, u32[]{:S(2)}) collective-permute-start(bf16[2,1,128,128]{3,2,1,0:T(8,128)(2,1)} %get-tuple-element.106), channel_id=1, source_target_pairs={{0,2},{2,4},{4,6},{6,8},{8,10},{10,12},{12,14},{14,0},{1,3},{3,5},... | collective-permute-start | bytes 196616 | tf_op jit(solution)/shard_map/ppermute | solution.py:16
  69.8 10.9 %collective-permute-start.5 = (bf16[1,6,128,128]{3,2,1,0:T(8,128)(2,1)}, bf16[1,6,128,128]{3,2,1,0:T(8,128)(2,1)}, u32[]{:S(2)}, u32[]{:S(2)}) collective-permute-start(bf16[1,6,128,128]{3,2,1,0:T(8,128)(2,1)} %get-tuple-element.97), channel_id=1, source_target_pairs={{16,0},{32,16},{48,32},{64,48},{80,64},{96,80},{112,96},{128,112},... | collective-permute-start | bytes 589832 | tf_op jit(solution)/shard_map/ppermute | solution.py:19
  118.5 10.9 %collective-permute-start.9 = (bf16[1,6,128,128]{3,2,1,0:T(8,128)(2,1)S(1)}, bf16[1,6,128,128]{3,2,1,0:T(8,128)(2,1)}, u32[]{:S(2)}, u32[]{:S(2)}) collective-permute-start(bf16[1,6,128,128]{3,2,1,0:T(8,128)(2,1)S(1)} %get-tuple-element.89), channel_id=1, source_target_pairs={{16,0},{32,16},{48,32},{64,48},{80,64},{96,80},{112,96},{128,112},... | collective-permute-start | bytes 589832 | tf_op jit(solution)/shard_map/ppermute | solution.py:19
  167.5 10.9 %collective-permute-start.13 = (bf16[1,6,128,128]{3,2,1,0:T(8,128)(2,1)}, bf16[1,6,128,128]{3,2,1,0:T(8,128)(2,1)}, u32[]{:S(2)}, u32[]{:S(2)}) collective-permute-start(bf16[1,6,128,128]{3,2,1,0:T(8,128)(2,1)} %get-tuple-element.81), channel_id=1, source_target_pairs={{16,0},{32,16},{48,32},{64,48},{80,64},{96,80},{112,96},{128,112},... | collective-permute-start | bytes 589832 | tf_op jit(solution)/shard_map/ppermute | solution.py:19
  186.6 13.6 %collective-permute-done.15 = bf16[2,1,128,128]{3,2,1,0:T(8,128)(2,1)} collective-permute-done((bf16[2,1,128,128]{3,2,1,0:T(8,128)(2,1)}, bf16[2,1,128,128]{3,2,1,0:T(8,128)(2,1)}, u32[]{:S(2)}, u32[]{:S(2)}) %collective-permute-start.15) | collective-permute-done | bytes 65568 | tf_op jit(solution)/shard_map/ppermute | solution.py:19
  214.5 10.9 %collective-permute-start.17 = (bf16[1,6,128,128]{3,2,1,0:T(8,128)(2,1)}, bf16[1,6,128,128]{3,2,1,0:T(8,128)(2,1)}, u32[]{:S(2)}, u32[]{:S(2)}) collective-permute-start(bf16[1,6,128,128]{3,2,1,0:T(8,128)(2,1)} %get-tuple-element.73), channel_id=1, source_target_pairs={{16,0},{32,16},{48,32},{64,48},{80,64},{96,80},{112,96},{128,112},... | collective-permute-start | bytes 589832 | tf_op jit(solution)/shard_map/ppermute | solution.py:19
  231.9 12.9 %collective-permute-done.19 = bf16[2,1,128,128]{3,2,1,0:T(8,128)(2,1)} collective-permute-done((bf16[2,1,128,128]{3,2,1,0:T(8,128)(2,1)}, bf16[2,1,128,128]{3,2,1,0:T(8,128)(2,1)}, u32[]{:S(2)}, u32[]{:S(2)}) %collective-permute-start.19) | collective-permute-done | bytes 65568 | tf_op jit(solution)/shard_map/ppermute | solution.py:19
  258.8 10.9 %collective-permute-start.21 = (bf16[1,6,128,128]{3,2,1,0:T(8,128)(2,1)}, bf16[1,6,128,128]{3,2,1,0:T(8,128)(2,1)}, u32[]{:S(2)}, u32[]{:S(2)}) collective-permute-start(bf16[1,6,128,128]{3,2,1,0:T(8,128)(2,1)} %get-tuple-element.65), channel_id=1, source_target_pairs={{16,0},{32,16},{48,32},{64,48},{80,64},{96,80},{112,96},{128,112},... | collective-permute-start | bytes 589832 | tf_op jit(solution)/shard_map/ppermute | solution.py:19
  278.1 10.3 %collective-permute-done.23 = bf16[2,1,128,128]{3,2,1,0:T(8,128)(2,1)} collective-permute-done((bf16[2,1,128,128]{3,2,1,0:T(8,128)(2,1)}, bf16[2,1,128,128]{3,2,1,0:T(8,128)(2,1)}, u32[]{:S(2)}, u32[]{:S(2)}) %collective-permute-start.23) | collective-permute-done | bytes 65568 | tf_op jit(solution)/shard_map/ppermute | solution.py:19
  303.8 10.9 %collective-permute-start.25 = (bf16[1,6,128,128]{3,2,1,0:T(8,128)(2,1)S(1)}, bf16[1,6,128,128]{3,2,1,0:T(8,128)(2,1)S(1)}, u32[]{:S(2)}, u32[]{:S(2)}) collective-permute-start(bf16[1,6,128,128]{3,2,1,0:T(8,128)(2,1)S(1)} %get-tuple-element.57), channel_id=1, source_target_pairs={{16,0},{32,16},{48,32},{64,48},{80,64},{96,80},{112,96},{128,112},... | collective-permute-start | bytes 589832 | tf_op jit(solution)/shard_map/ppermute | solution.py:19
  321.5 11.1 %collective-permute-done.27 = bf16[2,1,128,128]{3,2,1,0:T(8,128)(2,1)S(1)} collective-permute-done((bf16[2,1,128,128]{3,2,1,0:T(8,128)(2,1)S(1)}, bf16[2,1,128,128]{3,2,1,0:T(8,128)(2,1)S(1)}, u32[]{:S(2)}, u32[]{:S(2)}) %collective-permute-start.27) | collective-permute-done | bytes 65568 | tf_op jit(solution)/shard_map/ppermute | solution.py:19
  340.6 10.9 %collective-permute-start.29 = (bf16[1,6,128,128]{3,2,1,0:T(8,128)(2,1)S(1)}, bf16[1,6,128,128]{3,2,1,0:T(8,128)(2,1)S(1)}, u32[]{:S(2)}, u32[]{:S(2)}) collective-permute-start(bf16[1,6,128,128]{3,2,1,0:T(8,128)(2,1)S(1)} %get-tuple-element.49), channel_id=1, source_target_pairs={{16,0},{32,16},{48,32},{64,48},{80,64},{96,80},{112,96},{128,112},... | collective-permute-start | bytes 589832 | tf_op jit(solution)/shard_map/ppermute | solution.py:19
  358.2 11.2 %collective-permute-done.31 = bf16[2,1,128,128]{3,2,1,0:T(8,128)(2,1)S(1)} collective-permute-done((bf16[2,1,128,128]{3,2,1,0:T(8,128)(2,1)S(1)}, bf16[2,1,128,128]{3,2,1,0:T(8,128)(2,1)S(1)}, u32[]{:S(2)}, u32[]{:S(2)}) %collective-permute-start.31) | collective-permute-done | bytes 65568 | tf_op jit(solution)/shard_map/ppermute | solution.py:19
  380.6 10.9 %collective-permute-start.33 = (bf16[1,6,128,128]{3,2,1,0:T(8,128)(2,1)S(1)}, bf16[1,6,128,128]{3,2,1,0:T(8,128)(2,1)S(1)}, u32[]{:S(2)}, u32[]{:S(2)}) collective-permute-start(bf16[1,6,128,128]{3,2,1,0:T(8,128)(2,1)S(1)} %get-tuple-element.41), channel_id=1, source_target_pairs={{16,0},{32,16},{48,32},{64,48},{80,64},{96,80},{112,96},{128,112},... | collective-permute-start | bytes 589832 | tf_op jit(solution)/shard_map/ppermute | solution.py:19
  398.0 11.3 %collective-permute-done.35 = bf16[2,1,128,128]{3,2,1,0:T(8,128)(2,1)S(1)} collective-permute-done((bf16[2,1,128,128]{3,2,1,0:T(8,128)(2,1)S(1)}, bf16[2,1,128,128]{3,2,1,0:T(8,128)(2,1)S(1)}, u32[]{:S(2)}, u32[]{:S(2)}) %collective-permute-start.35) | collective-permute-done | bytes 65568 | tf_op jit(solution)/shard_map/ppermute | solution.py:19
  422.1 10.9 %collective-permute-start.37 = (bf16[1,6,128,128]{3,2,1,0:T(8,128)(2,1)S(1)}, bf16[1,6,128,128]{3,2,1,0:T(8,128)(2,1)S(1)}, u32[]{:S(2)}, u32[]{:S(2)}) collective-permute-start(bf16[1,6,128,128]{3,2,1,0:T(8,128)(2,1)S(1)} %get-tuple-element.33), channel_id=1, source_target_pairs={{16,0},{32,16},{48,32},{64,48},{80,64},{96,80},{112,96},{128,112},... | collective-permute-start | bytes 589832 | tf_op jit(solution)/shard_map/ppermute | solution.py:19
  439.6 11.1 %collective-permute-done.39 = bf16[2,1,128,128]{3,2,1,0:T(8,128)(2,1)S(1)} collective-permute-done((bf16[2,1,128,128]{3,2,1,0:T(8,128)(2,1)S(1)}, bf16[2,1,128,128]{3,2,1,0:T(8,128)(2,1)S(1)}, u32[]{:S(2)}, u32[]{:S(2)}) %collective-permute-start.39) | collective-permute-done | bytes 65568 | tf_op jit(solution)/shard_map/ppermute | solution.py:19
  465.1 10.9 %collective-permute-start.41 = (bf16[1,6,128,128]{3,2,1,0:T(8,128)(2,1)S(1)}, bf16[1,6,128,128]{3,2,1,0:T(8,128)(2,1)S(1)}, u32[]{:S(2)}, u32[]{:S(2)}) collective-permute-start(bf16[1,6,128,128]{3,2,1,0:T(8,128)(2,1)S(1)} %get-tuple-element.25), channel_id=1, source_target_pairs={{16,0},{32,16},{48,32},{64,48},{80,64},{96,80},{112,96},{128,112},... | collective-permute-start | bytes 589832 | tf_op jit(solution)/shard_map/ppermute | solution.py:19
  481.8 11.9 %collective-permute-done.43 = bf16[2,1,128,128]{3,2,1,0:T(8,128)(2,1)S(1)} collective-permute-done((bf16[2,1,128,128]{3,2,1,0:T(8,128)(2,1)S(1)}, bf16[2,1,128,128]{3,2,1,0:T(8,128)(2,1)S(1)}, u32[]{:S(2)}, u32[]{:S(2)}) %collective-permute-start.43) | collective-permute-done | bytes 65568 | tf_op jit(solution)/shard_map/ppermute | solution.py:19
  506.4 10.9 %collective-permute-start.45 = (bf16[1,6,128,128]{3,2,1,0:T(8,128)(2,1)S(1)}, bf16[1,6,128,128]{3,2,1,0:T(8,128)(2,1)S(1)}, u32[]{:S(2)}, u32[]{:S(2)}) collective-permute-start(bf16[1,6,128,128]{3,2,1,0:T(8,128)(2,1)S(1)} %get-tuple-element.17), channel_id=1, source_target_pairs={{16,0},{32,16},{48,32},{64,48},{80,64},{96,80},{112,96},{128,112},... | collective-permute-start | bytes 589832 | tf_op jit(solution)/shard_map/ppermute | solution.py:19
  523.2 12.0 %collective-permute-done.47 = bf16[2,1,128,128]{3,2,1,0:T(8,128)(2,1)S(1)} collective-permute-done((bf16[2,1,128,128]{3,2,1,0:T(8,128)(2,1)S(1)}, bf16[2,1,128,128]{3,2,1,0:T(8,128)(2,1)S(1)}, u32[]{:S(2)}, u32[]{:S(2)}) %collective-permute-start.47) | collective-permute-done | bytes 65568 | tf_op jit(solution)/shard_map/ppermute | solution.py:19
  547.0 10.9 %collective-permute-start.49 = (bf16[1,6,128,128]{3,2,1,0:T(8,128)(2,1)S(1)}, bf16[1,6,128,128]{3,2,1,0:T(8,128)(2,1)S(1)}, u32[]{:S(2)}, u32[]{:S(2)}) collective-permute-start(bf16[1,6,128,128]{3,2,1,0:T(8,128)(2,1)S(1)} %get-tuple-element.9), channel_id=1, source_target_pairs={{16,0},{32,16},{48,32},{64,48},{80,64},{96,80},{112,96},{128,112},... | collective-permute-start | bytes 589832 | tf_op jit(solution)/shard_map/ppermute | solution.py:19
  563.7 11.9 %collective-permute-done.51 = bf16[2,1,128,128]{3,2,1,0:T(8,128)(2,1)S(1)} collective-permute-done((bf16[2,1,128,128]{3,2,1,0:T(8,128)(2,1)S(1)}, bf16[2,1,128,128]{3,2,1,0:T(8,128)(2,1)S(1)}, u32[]{:S(2)}, u32[]{:S(2)}) %collective-permute-start.51) | collective-permute-done | bytes 65568 | tf_op jit(solution)/shard_map/ppermute | solution.py:19
  (327 shorter events, 310.4 us)
Async XLA Ops:
  10.8 45.0 %collective-permute-start = (bf16[1,6,128,128]{3,2,1,0:T(8,128)(2,1)}, bf16[1,6,128,128]{3,2,1,0:T(8,128)(2,1)S(1)}, u32[]{:S(2)}, u32[]{:S(2)}) collective-permute-start(bf16[1,6,128,128]{3,2,1,0:T(8,128)(2,1)} %get-tuple-element.104), channel_id=1, source_target_pairs={{0,16},{16,32},{32,48},{48,64},{64,80},{80,96},{96,112},{112,128},... | collective-permute-start | bytes 589832 | tf_op jit(solution)/shard_map/ppermute | solution.py:16
  14.3 41.4 %collective-permute-start.1 = (bf16[1,6,128,128]{3,2,1,0:T(8,128)(2,1)}, bf16[1,6,128,128]{3,2,1,0:T(8,128)(2,1)S(1)}, u32[]{:S(2)}, u32[]{:S(2)}) collective-permute-start(bf16[1,6,128,128]{3,2,1,0:T(8,128)(2,1)} %get-tuple-element.105), channel_id=1, source_target_pairs={{16,0},{32,16},{48,32},{64,48},{80,64},{96,80},{112,96},{128,112},... | collective-permute-start | bytes 589832 | tf_op jit(solution)/shard_map/ppermute | solution.py:19
  67.9 37.4 %collective-permute-start.4 = (bf16[1,6,128,128]{3,2,1,0:T(8,128)(2,1)}, bf16[1,6,128,128]{3,2,1,0:T(8,128)(2,1)S(1)}, u32[]{:S(2)}, u32[]{:S(2)}) collective-permute-start(bf16[1,6,128,128]{3,2,1,0:T(8,128)(2,1)} %get-tuple-element.96), channel_id=1, source_target_pairs={{0,16},{16,32},{32,48},{48,64},{64,80},{80,96},{96,112},{112,128},... | collective-permute-start | bytes 589832 | tf_op jit(solution)/shard_map/ppermute | solution.py:16
  69.8 35.5 %collective-permute-start.5 = (bf16[1,6,128,128]{3,2,1,0:T(8,128)(2,1)}, bf16[1,6,128,128]{3,2,1,0:T(8,128)(2,1)}, u32[]{:S(2)}, u32[]{:S(2)}) collective-permute-start(bf16[1,6,128,128]{3,2,1,0:T(8,128)(2,1)} %get-tuple-element.97), channel_id=1, source_target_pairs={{16,0},{32,16},{48,32},{64,48},{80,64},{96,80},{112,96},{128,112},... | collective-permute-start | bytes 589832 | tf_op jit(solution)/shard_map/ppermute | solution.py:19
  116.6 35.3 %collective-permute-start.8 = (bf16[1,6,128,128]{3,2,1,0:T(8,128)(2,1)}, bf16[1,6,128,128]{3,2,1,0:T(8,128)(2,1)S(1)}, u32[]{:S(2)}, u32[]{:S(2)}) collective-permute-start(bf16[1,6,128,128]{3,2,1,0:T(8,128)(2,1)} %get-tuple-element.88), channel_id=1, source_target_pairs={{0,16},{16,32},{32,48},{48,64},{64,80},{80,96},{96,112},{112,128},... | collective-permute-start | bytes 589832 | tf_op jit(solution)/shard_map/ppermute | solution.py:16
  118.5 34.0 %collective-permute-start.9 = (bf16[1,6,128,128]{3,2,1,0:T(8,128)(2,1)S(1)}, bf16[1,6,128,128]{3,2,1,0:T(8,128)(2,1)}, u32[]{:S(2)}, u32[]{:S(2)}) collective-permute-start(bf16[1,6,128,128]{3,2,1,0:T(8,128)(2,1)S(1)} %get-tuple-element.89), channel_id=1, source_target_pairs={{16,0},{32,16},{48,32},{64,48},{80,64},{96,80},{112,96},{128,112},... | collective-permute-start | bytes 589832 | tf_op jit(solution)/shard_map/ppermute | solution.py:19
  165.6 34.7 %collective-permute-start.12 = (bf16[1,6,128,128]{3,2,1,0:T(8,128)(2,1)}, bf16[1,6,128,128]{3,2,1,0:T(8,128)(2,1)S(1)}, u32[]{:S(2)}, u32[]{:S(2)}) collective-permute-start(bf16[1,6,128,128]{3,2,1,0:T(8,128)(2,1)} %get-tuple-element.80), channel_id=1, source_target_pairs={{0,16},{16,32},{32,48},{48,64},{64,80},{80,96},{96,112},{112,128},... | collective-permute-start | bytes 589832 | tf_op jit(solution)/shard_map/ppermute | solution.py:16
  167.5 32.8 %collective-permute-start.13 = (bf16[1,6,128,128]{3,2,1,0:T(8,128)(2,1)}, bf16[1,6,128,128]{3,2,1,0:T(8,128)(2,1)}, u32[]{:S(2)}, u32[]{:S(2)}) collective-permute-start(bf16[1,6,128,128]{3,2,1,0:T(8,128)(2,1)} %get-tuple-element.81), channel_id=1, source_target_pairs={{16,0},{32,16},{48,32},{64,48},{80,64},{96,80},{112,96},{128,112},... | collective-permute-start | bytes 589832 | tf_op jit(solution)/shard_map/ppermute | solution.py:19
  212.6 32.2 %collective-permute-start.16 = (bf16[1,6,128,128]{3,2,1,0:T(8,128)(2,1)}, bf16[1,6,128,128]{3,2,1,0:T(8,128)(2,1)S(1)}, u32[]{:S(2)}, u32[]{:S(2)}) collective-permute-start(bf16[1,6,128,128]{3,2,1,0:T(8,128)(2,1)} %get-tuple-element.72), channel_id=1, source_target_pairs={{0,16},{16,32},{32,48},{48,64},{64,80},{80,96},{96,112},{112,128},... | collective-permute-start | bytes 589832 | tf_op jit(solution)/shard_map/ppermute | solution.py:16
  214.5 30.3 %collective-permute-start.17 = (bf16[1,6,128,128]{3,2,1,0:T(8,128)(2,1)}, bf16[1,6,128,128]{3,2,1,0:T(8,128)(2,1)}, u32[]{:S(2)}, u32[]{:S(2)}) collective-permute-start(bf16[1,6,128,128]{3,2,1,0:T(8,128)(2,1)} %get-tuple-element.73), channel_id=1, source_target_pairs={{16,0},{32,16},{48,32},{64,48},{80,64},{96,80},{112,96},{128,112},... | collective-permute-start | bytes 589832 | tf_op jit(solution)/shard_map/ppermute | solution.py:19
  256.8 31.5 %collective-permute-start.20 = (bf16[1,6,128,128]{3,2,1,0:T(8,128)(2,1)}, bf16[1,6,128,128]{3,2,1,0:T(8,128)(2,1)S(1)}, u32[]{:S(2)}, u32[]{:S(2)}) collective-permute-start(bf16[1,6,128,128]{3,2,1,0:T(8,128)(2,1)} %get-tuple-element.64), channel_id=1, source_target_pairs={{0,16},{16,32},{32,48},{48,64},{64,80},{80,96},{96,112},{112,128},... | collective-permute-start | bytes 589832 | tf_op jit(solution)/shard_map/ppermute | solution.py:16
  258.8 29.6 %collective-permute-start.21 = (bf16[1,6,128,128]{3,2,1,0:T(8,128)(2,1)}, bf16[1,6,128,128]{3,2,1,0:T(8,128)(2,1)}, u32[]{:S(2)}, u32[]{:S(2)}) collective-permute-start(bf16[1,6,128,128]{3,2,1,0:T(8,128)(2,1)} %get-tuple-element.65), channel_id=1, source_target_pairs={{16,0},{32,16},{48,32},{64,48},{80,64},{96,80},{112,96},{128,112},... | collective-permute-start | bytes 589832 | tf_op jit(solution)/shard_map/ppermute | solution.py:19
  301.9 30.7 %collective-permute-start.24 = (bf16[1,6,128,128]{3,2,1,0:T(8,128)(2,1)S(1)}, bf16[1,6,128,128]{3,2,1,0:T(8,128)(2,1)S(1)}, u32[]{:S(2)}, u32[]{:S(2)}) collective-permute-start(bf16[1,6,128,128]{3,2,1,0:T(8,128)(2,1)S(1)} %get-tuple-element.56), channel_id=1, source_target_pairs={{0,16},{16,32},{32,48},{48,64},{64,80},{80,96},{96,112},{112,128},... | collective-permute-start | bytes 589832 | tf_op jit(solution)/shard_map/ppermute | solution.py:16
  338.7 30.7 %collective-permute-start.28 = (bf16[1,6,128,128]{3,2,1,0:T(8,128)(2,1)S(1)}, bf16[1,6,128,128]{3,2,1,0:T(8,128)(2,1)S(1)}, u32[]{:S(2)}, u32[]{:S(2)}) collective-permute-start(bf16[1,6,128,128]{3,2,1,0:T(8,128)(2,1)S(1)} %get-tuple-element.48), channel_id=1, source_target_pairs={{0,16},{16,32},{32,48},{48,64},{64,80},{80,96},{96,112},{112,128},... | collective-permute-start | bytes 589832 | tf_op jit(solution)/shard_map/ppermute | solution.py:16
  340.6 28.8 %collective-permute-start.29 = (bf16[1,6,128,128]{3,2,1,0:T(8,128)(2,1)S(1)}, bf16[1,6,128,128]{3,2,1,0:T(8,128)(2,1)S(1)}, u32[]{:S(2)}, u32[]{:S(2)}) collective-permute-start(bf16[1,6,128,128]{3,2,1,0:T(8,128)(2,1)S(1)} %get-tuple-element.49), channel_id=1, source_target_pairs={{16,0},{32,16},{48,32},{64,48},{80,64},{96,80},{112,96},{128,112},... | collective-permute-start | bytes 589832 | tf_op jit(solution)/shard_map/ppermute | solution.py:19
  378.7 30.6 %collective-permute-start.32 = (bf16[1,6,128,128]{3,2,1,0:T(8,128)(2,1)S(1)}, bf16[1,6,128,128]{3,2,1,0:T(8,128)(2,1)S(1)}, u32[]{:S(2)}, u32[]{:S(2)}) collective-permute-start(bf16[1,6,128,128]{3,2,1,0:T(8,128)(2,1)S(1)} %get-tuple-element.40), channel_id=1, source_target_pairs={{0,16},{16,32},{32,48},{48,64},{64,80},{80,96},{96,112},{112,128},... | collective-permute-start | bytes 589832 | tf_op jit(solution)/shard_map/ppermute | solution.py:16
  380.6 29.3 %collective-permute-start.33 = (bf16[1,6,128,128]{3,2,1,0:T(8,128)(2,1)S(1)}, bf16[1,6,128,128]{3,2,1,0:T(8,128)(2,1)S(1)}, u32[]{:S(2)}, u32[]{:S(2)}) collective-permute-start(bf16[1,6,128,128]{3,2,1,0:T(8,128)(2,1)S(1)} %get-tuple-element.41), channel_id=1, source_target_pairs={{16,0},{32,16},{48,32},{64,48},{80,64},{96,80},{112,96},{128,112},... | collective-permute-start | bytes 589832 | tf_op jit(solution)/shard_map/ppermute | solution.py:19
  420.2 30.6 %collective-permute-start.36 = (bf16[1,6,128,128]{3,2,1,0:T(8,128)(2,1)S(1)}, bf16[1,6,128,128]{3,2,1,0:T(8,128)(2,1)S(1)}, u32[]{:S(2)}, u32[]{:S(2)}) collective-permute-start(bf16[1,6,128,128]{3,2,1,0:T(8,128)(2,1)S(1)} %get-tuple-element.32), channel_id=1, source_target_pairs={{0,16},{16,32},{32,48},{48,64},{64,80},{80,96},{96,112},{112,128},... | collective-permute-start | bytes 589832 | tf_op jit(solution)/shard_map/ppermute | solution.py:16
  422.1 29.3 %collective-permute-start.37 = (bf16[1,6,128,128]{3,2,1,0:T(8,128)(2,1)S(1)}, bf16[1,6,128,128]{3,2,1,0:T(8,128)(2,1)S(1)}, u32[]{:S(2)}, u32[]{:S(2)}) collective-permute-start(bf16[1,6,128,128]{3,2,1,0:T(8,128)(2,1)S(1)} %get-tuple-element.33), channel_id=1, source_target_pairs={{16,0},{32,16},{48,32},{64,48},{80,64},{96,80},{112,96},{128,112},... | collective-permute-start | bytes 589832 | tf_op jit(solution)/shard_map/ppermute | solution.py:19
  463.1 30.6 %collective-permute-start.40 = (bf16[1,6,128,128]{3,2,1,0:T(8,128)(2,1)S(1)}, bf16[1,6,128,128]{3,2,1,0:T(8,128)(2,1)S(1)}, u32[]{:S(2)}, u32[]{:S(2)}) collective-permute-start(bf16[1,6,128,128]{3,2,1,0:T(8,128)(2,1)S(1)} %get-tuple-element.24), channel_id=1, source_target_pairs={{0,16},{16,32},{32,48},{48,64},{64,80},{80,96},{96,112},{112,128},... | collective-permute-start | bytes 589832 | tf_op jit(solution)/shard_map/ppermute | solution.py:16
  465.1 29.3 %collective-permute-start.41 = (bf16[1,6,128,128]{3,2,1,0:T(8,128)(2,1)S(1)}, bf16[1,6,128,128]{3,2,1,0:T(8,128)(2,1)S(1)}, u32[]{:S(2)}, u32[]{:S(2)}) collective-permute-start(bf16[1,6,128,128]{3,2,1,0:T(8,128)(2,1)S(1)} %get-tuple-element.25), channel_id=1, source_target_pairs={{16,0},{32,16},{48,32},{64,48},{80,64},{96,80},{112,96},{128,112},... | collective-permute-start | bytes 589832 | tf_op jit(solution)/shard_map/ppermute | solution.py:19
  504.5 30.7 %collective-permute-start.44 = (bf16[1,6,128,128]{3,2,1,0:T(8,128)(2,1)S(1)}, bf16[1,6,128,128]{3,2,1,0:T(8,128)(2,1)S(1)}, u32[]{:S(2)}, u32[]{:S(2)}) collective-permute-start(bf16[1,6,128,128]{3,2,1,0:T(8,128)(2,1)S(1)} %get-tuple-element.16), channel_id=1, source_target_pairs={{0,16},{16,32},{32,48},{48,64},{64,80},{80,96},{96,112},{112,128},... | collective-permute-start | bytes 589832 | tf_op jit(solution)/shard_map/ppermute | solution.py:16
  506.4 29.4 %collective-permute-start.45 = (bf16[1,6,128,128]{3,2,1,0:T(8,128)(2,1)S(1)}, bf16[1,6,128,128]{3,2,1,0:T(8,128)(2,1)S(1)}, u32[]{:S(2)}, u32[]{:S(2)}) collective-permute-start(bf16[1,6,128,128]{3,2,1,0:T(8,128)(2,1)S(1)} %get-tuple-element.17), channel_id=1, source_target_pairs={{16,0},{32,16},{48,32},{64,48},{80,64},{96,80},{112,96},{128,112},... | collective-permute-start | bytes 589832 | tf_op jit(solution)/shard_map/ppermute | solution.py:19
  545.0 30.6 %collective-permute-start.48 = (bf16[1,6,128,128]{3,2,1,0:T(8,128)(2,1)S(1)}, bf16[1,6,128,128]{3,2,1,0:T(8,128)(2,1)S(1)}, u32[]{:S(2)}, u32[]{:S(2)}) collective-permute-start(bf16[1,6,128,128]{3,2,1,0:T(8,128)(2,1)S(1)} %get-tuple-element.8), channel_id=1, source_target_pairs={{0,16},{16,32},{32,48},{48,64},{64,80},{80,96},{96,112},{112,128},... | collective-permute-start | bytes 589832 | tf_op jit(solution)/shard_map/ppermute | solution.py:16
  (68 other events, 765.3 us)
where the time goes:
time: 588 us; the launch traced here: 585 us
  starting transfers between devices  255 us (43%)
  waiting for transfers between devices  139 us (24%)
  local copies, waits for them, and re-layouts  85 us (14%)
  blocking collectives  54.2 us (9%)
  other arithmetic  31.5 us (5%)
  matrix products  17.9 us (3%)
    ppermute x26, starting transfers between devices, with_halo(): lax.ppermute(lax.slice_in_dim(block, 0, width, axis=dim), axis, backward)  180 us
    ppermute x26, waiting for transfers between devices, with_halo(): lax.ppermute(lax.slice_in_dim(block, 0, width, axis=dim), axis, backward)  139 us
    ppermute x26, starting transfers between devices, with_halo(): lax.ppermute(lax.slice_in_dim(block, block.shape[dim] - width, None, axis...  75.3 us
    all_gather x14, blocking collectives, pivot_apply(): whole_tile = lax.all_gather(carried, 'rad', axis=2, tiled=True)  51.8 us
    another operation x12, other arithmetic, neighbours_whole(): jnp.stack([lower_axial, upper_axial, lower_circ, upper_circ], axis=2)  16.2 us
    gather x6, local copies, waits for them, and re-layouts, apply_inverse(): beside = neighbours_sweep(backward)[chosen]  14.4 us
    dot_general x13, matrix products, couple(): jnp.einsum('tdkx,tdxc->tkc', masked, weight_rows, preferred_element_type=...  13.7 us
    gather x6, local copies, waits for them, and re-layouts, apply_inverse(): beside = neighbours_sweep(forward)[chosen]  13.1 us
  transfers between devices with their start and end apart: 52, of which 13 were waited for; matrix products, arithmetic and copies ran while one was open for 6% of the time, Pallas kernels for 0%

commit v1 on v0

--- a/solution.py
+++ b/solution.py
@@ -1,6 +1,8 @@
 import jax
 import jax.numpy as jnp
 from jax import lax
+from jax.experimental import pallas as pl
+from jax.experimental.pallas import tpu as pltpu
 from jax.sharding import PartitionSpec as P
 
 NLEV = 4
@@ -83,7 +85,7 @@
         return backward
 
     first_vector = apply_inverse(rhs_flat)
-    whole_first = lax.all_gather(first_vector, "rad", axis=2, tiled=True)
+    whole_first = gather_layers(first_vector)
     own_part = jnp.einsum(
         "tkx,txc->tkc", whole_first, diagonals, preferred_element_type=jnp.float32
     )
@@ -93,6 +95,29 @@
     second_vector = apply_inverse(operator_image)
     out_shape = (tiles_axial, tiles_circ, rhs_count, cell_count)
     return (first_vector.reshape(out_shape), second_vector.reshape(out_shape))
+
+
+def swap_kernel(x_ref, o_ref, send_sem, recv_sem):
+    other = {"rad": 1 - lax.axis_index("rad")}
+    barrier = pltpu.get_barrier_semaphore()
+    pl.semaphore_signal(barrier, inc=1, device_id=other, device_id_type=pl.DeviceIdType.MESH)
+    pl.semaphore_wait(barrier, 1)
+    copy = pltpu.make_async_remote_copy(x_ref, o_ref, send_sem, recv_sem, device_id=other, device_id_type=pl.DeviceIdType.MESH)
+    copy.start()
+    copy.wait()
+
+
+def gather_layers(x):
+    other = pl.pallas_call(
+        swap_kernel,
+        out_shape=jax.ShapeDtypeStruct(x.shape, x.dtype),
+        in_specs=[pl.BlockSpec(memory_space=pltpu.VMEM)],
+        out_specs=pl.BlockSpec(memory_space=pltpu.VMEM),
+        scratch_shapes=[pltpu.SemaphoreType.DMA, pltpu.SemaphoreType.DMA],
+        compiler_params=pltpu.CompilerParams(collective_id=0, has_side_effects=True),
+    )(x)
+    first = lax.axis_index("rad") == 0
+    return jnp.concatenate([jnp.where(first, x, other), jnp.where(first, other, x)], axis=2)
 
 
 def solution(mesh):

time: 588 us -> 589 us (level)
  no operation moved by 1% of the time
where the time goes in v1:
time: 589 us; the launch traced here: 586 us
  starting transfers between devices  255 us (43%)
  waiting for transfers between devices  138 us (23%)
  local copies, waits for them, and re-layouts  85.5 us (15%)
  blocking collectives  52.1 us (9%)
  other arithmetic  31.9 us (5%)
  matrix products  16.3 us (3%)
    ppermute x26, starting transfers between devices, with_halo(): lax.ppermute(lax.slice_in_dim(block, 0, width, axis=dim), axis, backward)  179 us
    ppermute x26, waiting for transfers between devices, with_halo(): lax.ppermute(lax.slice_in_dim(block, 0, width, axis=dim), axis, backward)  138 us
    ppermute x26, starting transfers between devices, with_halo(): lax.ppermute(lax.slice_in_dim(block, block.shape[dim] - width, None, axis...  75.7 us
    all_gather x14, blocking collectives, pivot_apply(): whole_tile = lax.all_gather(carried, 'rad', axis=2, tiled=True)  52.1 us
    another operation x12, other arithmetic, neighbours_whole(): jnp.stack([lower_axial, upper_axial, lower_circ, upper_circ], axis=2)  16.2 us
    gather x6, local copies, waits for them, and re-layouts, apply_inverse(): beside = neighbours_sweep(backward)[chosen]  13.6 us
    gather x6, local copies, waits for them, and re-layouts, apply_inverse(): beside = neighbours_sweep(forward)[chosen]  13.1 us
    gather x8, local copies, waits for them, and re-layouts, apply_inverse(): carried = source[chosen].astype(jnp.float32)  12.5 us
  transfers between devices with their start and end apart: 52, of which 13 were waited for; matrix products, arithmetic and copies ran while one was open for 6% of the time, Pallas kernels for 0%

profile of v1, /device:TPU:31, one launch (start us, length us, event | category | flops | bytes accessed | tf_op | source)
XLA Modules:
  0.0 585.8 jit_solution(14304363810510614461)
XLA Ops:
  14.4 11.4 %collective-permute-start.1 = (bf16[1,6,128,128]{3,2,1,0:T(8,128)(2,1)}, bf16[1,6,128,128]{3,2,1,0:T(8,128)(2,1)S(1)}, u32[]{:S(2)}, u32[]{:S(2)}) collective-permute-start(bf16[1,6,128,128]{3,2,1,0:T(8,128)(2,1)} %get-tuple-element.107), channel_id=1, source_target_pairs={{16,0},{32,16},{48,32},{64,48},{80,64},{96,80},{112,96},{128,112},... | collective-permute-start | bytes 589832 | tf_op jit(solution)/shard_map/ppermute | solution.py:21
  26.5 13.2 %collective-permute-start.2 = (bf16[2,1,128,128]{3,2,1,0:T(8,128)(2,1)}, bf16[2,1,128,128]{3,2,1,0:T(8,128)(2,1)}, u32[]{:S(2)}, u32[]{:S(2)}) collective-permute-start(bf16[2,1,128,128]{3,2,1,0:T(8,128)(2,1)} %get-tuple-element.108), channel_id=1, source_target_pairs={{0,2},{2,4},{4,6},{6,8},{8,10},{10,12},{12,14},{14,0},{1,3},{3,5},... | collective-permute-start | bytes 196616 | tf_op jit(solution)/shard_map/ppermute | solution.py:18
  69.9 10.9 %collective-permute-start.5 = (bf16[1,6,128,128]{3,2,1,0:T(8,128)(2,1)}, bf16[1,6,128,128]{3,2,1,0:T(8,128)(2,1)}, u32[]{:S(2)}, u32[]{:S(2)}) collective-permute-start(bf16[1,6,128,128]{3,2,1,0:T(8,128)(2,1)} %get-tuple-element.99), channel_id=1, source_target_pairs={{16,0},{32,16},{48,32},{64,48},{80,64},{96,80},{112,96},{128,112},... | collective-permute-start | bytes 589832 | tf_op jit(solution)/shard_map/ppermute | solution.py:21
  118.6 10.9 %collective-permute-start.9 = (bf16[1,6,128,128]{3,2,1,0:T(8,128)(2,1)S(1)}, bf16[1,6,128,128]{3,2,1,0:T(8,128)(2,1)}, u32[]{:S(2)}, u32[]{:S(2)}) collective-permute-start(bf16[1,6,128,128]{3,2,1,0:T(8,128)(2,1)S(1)} %get-tuple-element.91), channel_id=1, source_target_pairs={{16,0},{32,16},{48,32},{64,48},{80,64},{96,80},{112,96},{128,112},... | collective-permute-start | bytes 589832 | tf_op jit(solution)/shard_map/ppermute | solution.py:21
  167.6 10.9 %collective-permute-start.13 = (bf16[1,6,128,128]{3,2,1,0:T(8,128)(2,1)}, bf16[1,6,128,128]{3,2,1,0:T(8,128)(2,1)}, u32[]{:S(2)}, u32[]{:S(2)}) collective-permute-start(bf16[1,6,128,128]{3,2,1,0:T(8,128)(2,1)} %get-tuple-element.83), channel_id=1, source_target_pairs={{16,0},{32,16},{48,32},{64,48},{80,64},{96,80},{112,96},{128,112},... | collective-permute-start | bytes 589832 | tf_op jit(solution)/shard_map/ppermute | solution.py:21
  186.7 13.6 %collective-permute-done.15 = bf16[2,1,128,128]{3,2,1,0:T(8,128)(2,1)} collective-permute-done((bf16[2,1,128,128]{3,2,1,0:T(8,128)(2,1)}, bf16[2,1,128,128]{3,2,1,0:T(8,128)(2,1)}, u32[]{:S(2)}, u32[]{:S(2)}) %collective-permute-start.15) | collective-permute-done | bytes 65568 | tf_op jit(solution)/shard_map/ppermute | solution.py:21
  214.5 10.9 %collective-permute-start.17 = (bf16[1,6,128,128]{3,2,1,0:T(8,128)(2,1)}, bf16[1,6,128,128]{3,2,1,0:T(8,128)(2,1)}, u32[]{:S(2)}, u32[]{:S(2)}) collective-permute-start(bf16[1,6,128,128]{3,2,1,0:T(8,128)(2,1)} %get-tuple-element.75), channel_id=1, source_target_pairs={{16,0},{32,16},{48,32},{64,48},{80,64},{96,80},{112,96},{128,112},... | collective-permute-start | bytes 589832 | tf_op jit(solution)/shard_map/ppermute | solution.py:21
  232.0 12.9 %collective-permute-done.19 = bf16[2,1,128,128]{3,2,1,0:T(8,128)(2,1)} collective-permute-done((bf16[2,1,128,128]{3,2,1,0:T(8,128)(2,1)}, bf16[2,1,128,128]{3,2,1,0:T(8,128)(2,1)}, u32[]{:S(2)}, u32[]{:S(2)}) %collective-permute-start.19) | collective-permute-done | bytes 65568 | tf_op jit(solution)/shard_map/ppermute | solution.py:21
  258.8 10.9 %collective-permute-start.21 = (bf16[1,6,128,128]{3,2,1,0:T(8,128)(2,1)}, bf16[1,6,128,128]{3,2,1,0:T(8,128)(2,1)}, u32[]{:S(2)}, u32[]{:S(2)}) collective-permute-start(bf16[1,6,128,128]{3,2,1,0:T(8,128)(2,1)} %get-tuple-element.67), channel_id=1, source_target_pairs={{16,0},{32,16},{48,32},{64,48},{80,64},{96,80},{112,96},{128,112},... | collective-permute-start | bytes 589832 | tf_op jit(solution)/shard_map/ppermute | solution.py:21
  278.2 10.5 %collective-permute-done.23 = bf16[2,1,128,128]{3,2,1,0:T(8,128)(2,1)} collective-permute-done((bf16[2,1,128,128]{3,2,1,0:T(8,128)(2,1)}, bf16[2,1,128,128]{3,2,1,0:T(8,128)(2,1)}, u32[]{:S(2)}, u32[]{:S(2)}) %collective-permute-start.23) | collective-permute-done | bytes 65568 | tf_op jit(solution)/shard_map/ppermute | solution.py:21
  305.8 10.9 %collective-permute-start.25 = (bf16[1,6,128,128]{3,2,1,0:T(8,128)(2,1)}, bf16[1,6,128,128]{3,2,1,0:T(8,128)(2,1)S(1)}, u32[]{:S(2)}, u32[]{:S(2)}) collective-permute-start(bf16[1,6,128,128]{3,2,1,0:T(8,128)(2,1)} %get-tuple-element.59), channel_id=1, source_target_pairs={{16,0},{32,16},{48,32},{64,48},{80,64},{96,80},{112,96},{128,112},... | collective-permute-start | bytes 589832 | tf_op jit(solution)/shard_map/ppermute | solution.py:21
  325.6 10.1 %collective-permute-done.27 = bf16[2,1,128,128]{3,2,1,0:T(8,128)(2,1)S(1)} collective-permute-done((bf16[2,1,128,128]{3,2,1,0:T(8,128)(2,1)S(1)}, bf16[2,1,128,128]{3,2,1,0:T(8,128)(2,1)S(1)}, u32[]{:S(2)}, u32[]{:S(2)}) %collective-permute-start.27) | collective-permute-done | bytes 65568 | tf_op jit(solution)/shard_map/ppermute | solution.py:21
  344.2 10.9 %collective-permute-start.29 = (bf16[1,6,128,128]{3,2,1,0:T(8,128)(2,1)S(1)}, bf16[1,6,128,128]{3,2,1,0:T(8,128)(2,1)S(1)}, u32[]{:S(2)}, u32[]{:S(2)}) collective-permute-start(bf16[1,6,128,128]{3,2,1,0:T(8,128)(2,1)S(1)} %get-tuple-element.51), channel_id=1, source_target_pairs={{16,0},{32,16},{48,32},{64,48},{80,64},{96,80},{112,96},{128,112},... | collective-permute-start | bytes 589832 | tf_op jit(solution)/shard_map/ppermute | solution.py:21
  361.7 11.3 %collective-permute-done.31 = bf16[2,1,128,128]{3,2,1,0:T(8,128)(2,1)S(1)} collective-permute-done((bf16[2,1,128,128]{3,2,1,0:T(8,128)(2,1)S(1)}, bf16[2,1,128,128]{3,2,1,0:T(8,128)(2,1)S(1)}, u32[]{:S(2)}, u32[]{:S(2)}) %collective-permute-start.31) | collective-permute-done | bytes 65568 | tf_op jit(solution)/shard_map/ppermute | solution.py:21
  386.1 10.9 %collective-permute-start.33 = (bf16[1,6,128,128]{3,2,1,0:T(8,128)(2,1)S(1)}, bf16[1,6,128,128]{3,2,1,0:T(8,128)(2,1)S(1)}, u32[]{:S(2)}, u32[]{:S(2)}) collective-permute-start(bf16[1,6,128,128]{3,2,1,0:T(8,128)(2,1)S(1)} %get-tuple-element.43), channel_id=1, source_target_pairs={{16,0},{32,16},{48,32},{64,48},{80,64},{96,80},{112,96},{128,112},... | collective-permute-start | bytes 589832 | tf_op jit(solution)/shard_map/ppermute | solution.py:21
  403.4 11.3 %collective-permute-done.35 = bf16[2,1,128,128]{3,2,1,0:T(8,128)(2,1)S(1)} collective-permute-done((bf16[2,1,128,128]{3,2,1,0:T(8,128)(2,1)S(1)}, bf16[2,1,128,128]{3,2,1,0:T(8,128)(2,1)S(1)}, u32[]{:S(2)}, u32[]{:S(2)}) %collective-permute-start.35) | collective-permute-done | bytes 65568 | tf_op jit(solution)/shard_map/ppermute | solution.py:21
  427.6 10.9 %collective-permute-start.37 = (bf16[1,6,128,128]{3,2,1,0:T(8,128)(2,1)S(1)}, bf16[1,6,128,128]{3,2,1,0:T(8,128)(2,1)S(1)}, u32[]{:S(2)}, u32[]{:S(2)}) collective-permute-start(bf16[1,6,128,128]{3,2,1,0:T(8,128)(2,1)S(1)} %get-tuple-element.35), channel_id=1, source_target_pairs={{16,0},{32,16},{48,32},{64,48},{80,64},{96,80},{112,96},{128,112},... | collective-permute-start | bytes 589832 | tf_op jit(solution)/shard_map/ppermute | solution.py:21
  445.1 11.2 %collective-permute-done.39 = bf16[2,1,128,128]{3,2,1,0:T(8,128)(2,1)S(1)} collective-permute-done((bf16[2,1,128,128]{3,2,1,0:T(8,128)(2,1)S(1)}, bf16[2,1,128,128]{3,2,1,0:T(8,128)(2,1)S(1)}, u32[]{:S(2)}, u32[]{:S(2)}) %collective-permute-start.39) | collective-permute-done | bytes 65568 | tf_op jit(solution)/shard_map/ppermute | solution.py:21
  469.7 10.9 %collective-permute-start.41 = (bf16[1,6,128,128]{3,2,1,0:T(8,128)(2,1)S(1)}, bf16[1,6,128,128]{3,2,1,0:T(8,128)(2,1)S(1)}, u32[]{:S(2)}, u32[]{:S(2)}) collective-permute-start(bf16[1,6,128,128]{3,2,1,0:T(8,128)(2,1)S(1)} %get-tuple-element.27), channel_id=1, source_target_pairs={{16,0},{32,16},{48,32},{64,48},{80,64},{96,80},{112,96},{128,112},... | collective-permute-start | bytes 589832 | tf_op jit(solution)/shard_map/ppermute | solution.py:21
  486.5 12.1 %collective-permute-done.43 = bf16[2,1,128,128]{3,2,1,0:T(8,128)(2,1)S(1)} collective-permute-done((bf16[2,1,128,128]{3,2,1,0:T(8,128)(2,1)S(1)}, bf16[2,1,128,128]{3,2,1,0:T(8,128)(2,1)S(1)}, u32[]{:S(2)}, u32[]{:S(2)}) %collective-permute-start.43) | collective-permute-done | bytes 65568 | tf_op jit(solution)/shard_map/ppermute | solution.py:21
  508.9 10.9 %collective-permute-start.45 = (bf16[1,6,128,128]{3,2,1,0:T(8,128)(2,1)S(1)}, bf16[1,6,128,128]{3,2,1,0:T(8,128)(2,1)S(1)}, u32[]{:S(2)}, u32[]{:S(2)}) collective-permute-start(bf16[1,6,128,128]{3,2,1,0:T(8,128)(2,1)S(1)} %get-tuple-element.19), channel_id=1, source_target_pairs={{16,0},{32,16},{48,32},{64,48},{80,64},{96,80},{112,96},{128,112},... | collective-permute-start | bytes 589832 | tf_op jit(solution)/shard_map/ppermute | solution.py:21
  525.7 11.9 %collective-permute-done.47 = bf16[2,1,128,128]{3,2,1,0:T(8,128)(2,1)S(1)} collective-permute-done((bf16[2,1,128,128]{3,2,1,0:T(8,128)(2,1)S(1)}, bf16[2,1,128,128]{3,2,1,0:T(8,128)(2,1)S(1)}, u32[]{:S(2)}, u32[]{:S(2)}) %collective-permute-start.47) | collective-permute-done | bytes 65568 | tf_op jit(solution)/shard_map/ppermute | solution.py:21
  547.9 10.9 %collective-permute-start.49 = (bf16[1,6,128,128]{3,2,1,0:T(8,128)(2,1)S(1)}, bf16[1,6,128,128]{3,2,1,0:T(8,128)(2,1)S(1)}, u32[]{:S(2)}, u32[]{:S(2)}) collective-permute-start(bf16[1,6,128,128]{3,2,1,0:T(8,128)(2,1)S(1)} %get-tuple-element.11), channel_id=1, source_target_pairs={{16,0},{32,16},{48,32},{64,48},{80,64},{96,80},{112,96},{128,112},... | collective-permute-start | bytes 589832 | tf_op jit(solution)/shard_map/ppermute | solution.py:21
  564.7 11.9 %collective-permute-done.51 = bf16[2,1,128,128]{3,2,1,0:T(8,128)(2,1)S(1)} collective-permute-done((bf16[2,1,128,128]{3,2,1,0:T(8,128)(2,1)S(1)}, bf16[2,1,128,128]{3,2,1,0:T(8,128)(2,1)S(1)}, u32[]{:S(2)}, u32[]{:S(2)}) %collective-permute-start.51) | collective-permute-done | bytes 65568 | tf_op jit(solution)/shard_map/ppermute | solution.py:21
  (334 shorter events, 311.8 us)
Async XLA Ops:
  10.8 45.0 %collective-permute-start = (bf16[1,6,128,128]{3,2,1,0:T(8,128)(2,1)}, bf16[1,6,128,128]{3,2,1,0:T(8,128)(2,1)S(1)}, u32[]{:S(2)}, u32[]{:S(2)}) collective-permute-start(bf16[1,6,128,128]{3,2,1,0:T(8,128)(2,1)} %get-tuple-element.106), channel_id=1, source_target_pairs={{0,16},{16,32},{32,48},{48,64},{64,80},{80,96},{96,112},{112,128},... | collective-permute-start | bytes 589832 | tf_op jit(solution)/shard_map/ppermute | solution.py:18
  14.4 41.4 %collective-permute-start.1 = (bf16[1,6,128,128]{3,2,1,0:T(8,128)(2,1)}, bf16[1,6,128,128]{3,2,1,0:T(8,128)(2,1)S(1)}, u32[]{:S(2)}, u32[]{:S(2)}) collective-permute-start(bf16[1,6,128,128]{3,2,1,0:T(8,128)(2,1)} %get-tuple-element.107), channel_id=1, source_target_pairs={{16,0},{32,16},{48,32},{64,48},{80,64},{96,80},{112,96},{128,112},... | collective-permute-start | bytes 589832 | tf_op jit(solution)/shard_map/ppermute | solution.py:21
  67.9 37.4 %collective-permute-start.4 = (bf16[1,6,128,128]{3,2,1,0:T(8,128)(2,1)}, bf16[1,6,128,128]{3,2,1,0:T(8,128)(2,1)S(1)}, u32[]{:S(2)}, u32[]{:S(2)}) collective-permute-start(bf16[1,6,128,128]{3,2,1,0:T(8,128)(2,1)} %get-tuple-element.98), channel_id=1, source_target_pairs={{0,16},{16,32},{32,48},{48,64},{64,80},{80,96},{96,112},{112,128},... | collective-permute-start | bytes 589832 | tf_op jit(solution)/shard_map/ppermute | solution.py:18
  69.9 35.5 %collective-permute-start.5 = (bf16[1,6,128,128]{3,2,1,0:T(8,128)(2,1)}, bf16[1,6,128,128]{3,2,1,0:T(8,128)(2,1)}, u32[]{:S(2)}, u32[]{:S(2)}) collective-permute-start(bf16[1,6,128,128]{3,2,1,0:T(8,128)(2,1)} %get-tuple-element.99), channel_id=1, source_target_pairs={{16,0},{32,16},{48,32},{64,48},{80,64},{96,80},{112,96},{128,112},... | collective-permute-start | bytes 589832 | tf_op jit(solution)/shard_map/ppermute | solution.py:21
  116.6 35.3 %collective-permute-start.8 = (bf16[1,6,128,128]{3,2,1,0:T(8,128)(2,1)}, bf16[1,6,128,128]{3,2,1,0:T(8,128)(2,1)S(1)}, u32[]{:S(2)}, u32[]{:S(2)}) collective-permute-start(bf16[1,6,128,128]{3,2,1,0:T(8,128)(2,1)} %get-tuple-element.90), channel_id=1, source_target_pairs={{0,16},{16,32},{32,48},{48,64},{64,80},{80,96},{96,112},{112,128},... | collective-permute-start | bytes 589832 | tf_op jit(solution)/shard_map/ppermute | solution.py:18
  118.6 34.0 %collective-permute-start.9 = (bf16[1,6,128,128]{3,2,1,0:T(8,128)(2,1)S(1)}, bf16[1,6,128,128]{3,2,1,0:T(8,128)(2,1)}, u32[]{:S(2)}, u32[]{:S(2)}) collective-permute-start(bf16[1,6,128,128]{3,2,1,0:T(8,128)(2,1)S(1)} %get-tuple-element.91), channel_id=1, source_target_pairs={{16,0},{32,16},{48,32},{64,48},{80,64},{96,80},{112,96},{128,112},... | collective-permute-start | bytes 589832 | tf_op jit(solution)/shard_map/ppermute | solution.py:21
  165.7 34.7 %collective-permute-start.12 = (bf16[1,6,128,128]{3,2,1,0:T(8,128)(2,1)}, bf16[1,6,128,128]{3,2,1,0:T(8,128)(2,1)S(1)}, u32[]{:S(2)}, u32[]{:S(2)}) collective-permute-start(bf16[1,6,128,128]{3,2,1,0:T(8,128)(2,1)} %get-tuple-element.82), channel_id=1, source_target_pairs={{0,16},{16,32},{32,48},{48,64},{64,80},{80,96},{96,112},{112,128},... | collective-permute-start | bytes 589832 | tf_op jit(solution)/shard_map/ppermute | solution.py:18
  167.6 32.8 %collective-permute-start.13 = (bf16[1,6,128,128]{3,2,1,0:T(8,128)(2,1)}, bf16[1,6,128,128]{3,2,1,0:T(8,128)(2,1)}, u32[]{:S(2)}, u32[]{:S(2)}) collective-permute-start(bf16[1,6,128,128]{3,2,1,0:T(8,128)(2,1)} %get-tuple-element.83), channel_id=1, source_target_pairs={{16,0},{32,16},{48,32},{64,48},{80,64},{96,80},{112,96},{128,112},... | collective-permute-start | bytes 589832 | tf_op jit(solution)/shard_map/ppermute | solution.py:21
  212.6 32.2 %collective-permute-start.16 = (bf16[1,6,128,128]{3,2,1,0:T(8,128)(2,1)}, bf16[1,6,128,128]{3,2,1,0:T(8,128)(2,1)S(1)}, u32[]{:S(2)}, u32[]{:S(2)}) collective-permute-start(bf16[1,6,128,128]{3,2,1,0:T(8,128)(2,1)} %get-tuple-element.74), channel_id=1, source_target_pairs={{0,16},{16,32},{32,48},{48,64},{64,80},{80,96},{96,112},{112,128},... | collective-permute-start | bytes 589832 | tf_op jit(solution)/shard_map/ppermute | solution.py:18
  214.5 30.3 %collective-permute-start.17 = (bf16[1,6,128,128]{3,2,1,0:T(8,128)(2,1)}, bf16[1,6,128,128]{3,2,1,0:T(8,128)(2,1)}, u32[]{:S(2)}, u32[]{:S(2)}) collective-permute-start(bf16[1,6,128,128]{3,2,1,0:T(8,128)(2,1)} %get-tuple-element.75), channel_id=1, source_target_pairs={{16,0},{32,16},{48,32},{64,48},{80,64},{96,80},{112,96},{128,112},... | collective-permute-start | bytes 589832 | tf_op jit(solution)/shard_map/ppermute | solution.py:21
  256.9 31.8 %collective-permute-start.20 = (bf16[1,6,128,128]{3,2,1,0:T(8,128)(2,1)}, bf16[1,6,128,128]{3,2,1,0:T(8,128)(2,1)S(1)}, u32[]{:S(2)}, u32[]{:S(2)}) collective-permute-start(bf16[1,6,128,128]{3,2,1,0:T(8,128)(2,1)} %get-tuple-element.66), channel_id=1, source_target_pairs={{0,16},{16,32},{32,48},{48,64},{64,80},{80,96},{96,112},{112,128},... | collective-permute-start | bytes 589832 | tf_op jit(solution)/shard_map/ppermute | solution.py:18
  258.8 29.8 %collective-permute-start.21 = (bf16[1,6,128,128]{3,2,1,0:T(8,128)(2,1)}, bf16[1,6,128,128]{3,2,1,0:T(8,128)(2,1)}, u32[]{:S(2)}, u32[]{:S(2)}) collective-permute-start(bf16[1,6,128,128]{3,2,1,0:T(8,128)(2,1)} %get-tuple-element.67), channel_id=1, source_target_pairs={{16,0},{32,16},{48,32},{64,48},{80,64},{96,80},{112,96},{128,112},... | collective-permute-start | bytes 589832 | tf_op jit(solution)/shard_map/ppermute | solution.py:21
  303.9 31.9 %collective-permute-start.24 = (bf16[1,6,128,128]{3,2,1,0:T(8,128)(2,1)}, bf16[1,6,128,128]{3,2,1,0:T(8,128)(2,1)S(1)}, u32[]{:S(2)}, u32[]{:S(2)}) collective-permute-start(bf16[1,6,128,128]{3,2,1,0:T(8,128)(2,1)} %get-tuple-element.58), channel_id=1, source_target_pairs={{0,16},{16,32},{32,48},{48,64},{64,80},{80,96},{96,112},{112,128},... | collective-permute-start | bytes 589832 | tf_op jit(solution)/shard_map/ppermute | solution.py:18
  305.8 29.9 %collective-permute-start.25 = (bf16[1,6,128,128]{3,2,1,0:T(8,128)(2,1)}, bf16[1,6,128,128]{3,2,1,0:T(8,128)(2,1)S(1)}, u32[]{:S(2)}, u32[]{:S(2)}) collective-permute-start(bf16[1,6,128,128]{3,2,1,0:T(8,128)(2,1)} %get-tuple-element.59), channel_id=1, source_target_pairs={{16,0},{32,16},{48,32},{64,48},{80,64},{96,80},{112,96},{128,112},... | collective-permute-start | bytes 589832 | tf_op jit(solution)/shard_map/ppermute | solution.py:21
  342.3 30.8 %collective-permute-start.28 = (bf16[1,6,128,128]{3,2,1,0:T(8,128)(2,1)S(1)}, bf16[1,6,128,128]{3,2,1,0:T(8,128)(2,1)S(1)}, u32[]{:S(2)}, u32[]{:S(2)}) collective-permute-start(bf16[1,6,128,128]{3,2,1,0:T(8,128)(2,1)S(1)} %get-tuple-element.50), channel_id=1, source_target_pairs={{0,16},{16,32},{32,48},{48,64},{64,80},{80,96},{96,112},{112,128},... | collective-permute-start | bytes 589832 | tf_op jit(solution)/shard_map/ppermute | solution.py:18
  344.2 29.5 %collective-permute-start.29 = (bf16[1,6,128,128]{3,2,1,0:T(8,128)(2,1)S(1)}, bf16[1,6,128,128]{3,2,1,0:T(8,128)(2,1)S(1)}, u32[]{:S(2)}, u32[]{:S(2)}) collective-permute-start(bf16[1,6,128,128]{3,2,1,0:T(8,128)(2,1)S(1)} %get-tuple-element.51), channel_id=1, source_target_pairs={{16,0},{32,16},{48,32},{64,48},{80,64},{96,80},{112,96},{128,112},... | collective-permute-start | bytes 589832 | tf_op jit(solution)/shard_map/ppermute | solution.py:21
  384.1 30.6 %collective-permute-start.32 = (bf16[1,6,128,128]{3,2,1,0:T(8,128)(2,1)S(1)}, bf16[1,6,128,128]{3,2,1,0:T(8,128)(2,1)S(1)}, u32[]{:S(2)}, u32[]{:S(2)}) collective-permute-start(bf16[1,6,128,128]{3,2,1,0:T(8,128)(2,1)S(1)} %get-tuple-element.42), channel_id=1, source_target_pairs={{0,16},{16,32},{32,48},{48,64},{64,80},{80,96},{96,112},{112,128},... | collective-permute-start | bytes 589832 | tf_op jit(solution)/shard_map/ppermute | solution.py:18
  386.1 29.3 %collective-permute-start.33 = (bf16[1,6,128,128]{3,2,1,0:T(8,128)(2,1)S(1)}, bf16[1,6,128,128]{3,2,1,0:T(8,128)(2,1)S(1)}, u32[]{:S(2)}, u32[]{:S(2)}) collective-permute-start(bf16[1,6,128,128]{3,2,1,0:T(8,128)(2,1)S(1)} %get-tuple-element.43), channel_id=1, source_target_pairs={{16,0},{32,16},{48,32},{64,48},{80,64},{96,80},{112,96},{128,112},... | collective-permute-start | bytes 589832 | tf_op jit(solution)/shard_map/ppermute | solution.py:21
  425.6 30.6 %collective-permute-start.36 = (bf16[1,6,128,128]{3,2,1,0:T(8,128)(2,1)S(1)}, bf16[1,6,128,128]{3,2,1,0:T(8,128)(2,1)S(1)}, u32[]{:S(2)}, u32[]{:S(2)}) collective-permute-start(bf16[1,6,128,128]{3,2,1,0:T(8,128)(2,1)S(1)} %get-tuple-element.34), channel_id=1, source_target_pairs={{0,16},{16,32},{32,48},{48,64},{64,80},{80,96},{96,112},{112,128},... | collective-permute-start | bytes 589832 | tf_op jit(solution)/shard_map/ppermute | solution.py:18
  427.6 29.3 %collective-permute-start.37 = (bf16[1,6,128,128]{3,2,1,0:T(8,128)(2,1)S(1)}, bf16[1,6,128,128]{3,2,1,0:T(8,128)(2,1)S(1)}, u32[]{:S(2)}, u32[]{:S(2)}) collective-permute-start(bf16[1,6,128,128]{3,2,1,0:T(8,128)(2,1)S(1)} %get-tuple-element.35), channel_id=1, source_target_pairs={{16,0},{32,16},{48,32},{64,48},{80,64},{96,80},{112,96},{128,112},... | collective-permute-start | bytes 589832 | tf_op jit(solution)/shard_map/ppermute | solution.py:21
  467.8 30.8 %collective-permute-start.40 = (bf16[1,6,128,128]{3,2,1,0:T(8,128)(2,1)S(1)}, bf16[1,6,128,128]{3,2,1,0:T(8,128)(2,1)S(1)}, u32[]{:S(2)}, u32[]{:S(2)}) collective-permute-start(bf16[1,6,128,128]{3,2,1,0:T(8,128)(2,1)S(1)} %get-tuple-element.26), channel_id=1, source_target_pairs={{0,16},{16,32},{32,48},{48,64},{64,80},{80,96},{96,112},{112,128},... | collective-permute-start | bytes 589832 | tf_op jit(solution)/shard_map/ppermute | solution.py:18
  469.7 28.9 %collective-permute-start.41 = (bf16[1,6,128,128]{3,2,1,0:T(8,128)(2,1)S(1)}, bf16[1,6,128,128]{3,2,1,0:T(8,128)(2,1)S(1)}, u32[]{:S(2)}, u32[]{:S(2)}) collective-permute-start(bf16[1,6,128,128]{3,2,1,0:T(8,128)(2,1)S(1)} %get-tuple-element.27), channel_id=1, source_target_pairs={{16,0},{32,16},{48,32},{64,48},{80,64},{96,80},{112,96},{128,112},... | collective-permute-start | bytes 589832 | tf_op jit(solution)/shard_map/ppermute | solution.py:21
  507.0 30.6 %collective-permute-start.44 = (bf16[1,6,128,128]{3,2,1,0:T(8,128)(2,1)S(1)}, bf16[1,6,128,128]{3,2,1,0:T(8,128)(2,1)S(1)}, u32[]{:S(2)}, u32[]{:S(2)}) collective-permute-start(bf16[1,6,128,128]{3,2,1,0:T(8,128)(2,1)S(1)} %get-tuple-element.18), channel_id=1, source_target_pairs={{0,16},{16,32},{32,48},{48,64},{64,80},{80,96},{96,112},{112,128},... | collective-permute-start | bytes 589832 | tf_op jit(solution)/shard_map/ppermute | solution.py:18
  546.0 30.6 %collective-permute-start.48 = (bf16[1,6,128,128]{3,2,1,0:T(8,128)(2,1)S(1)}, bf16[1,6,128,128]{3,2,1,0:T(8,128)(2,1)S(1)}, u32[]{:S(2)}, u32[]{:S(2)}) collective-permute-start(bf16[1,6,128,128]{3,2,1,0:T(8,128)(2,1)S(1)} %get-tuple-element.10), channel_id=1, source_target_pairs={{0,16},{16,32},{32,48},{48,64},{64,80},{80,96},{96,112},{112,128},... | collective-permute-start | bytes 589832 | tf_op jit(solution)/shard_map/ppermute | solution.py:18
  (71 other events, 758.7 us)

commit v2 on v0

v2 whole, which is shorter than its diff:
```python
import functools

import jax
import jax.numpy as jnp
from jax import lax
from jax.experimental import pallas as pl
from jax.experimental.pallas import tpu as pltpu
from jax.sharding import PartitionSpec as P

MESH = pl.DeviceIdType.MESH
F32 = jnp.float32
BF16 = jnp.bfloat16
GROUPS = 2
NLEV = 4
LOW_AX, UP_AX, LOW_C, UP_C = range(4)
FIRST = (0, 3, 6, 7)
WIDTH = (3, 3, 1, 1)
SLOTS = 8


def kernel(
    n_ax,
    n_circ,
    rhs,
    pivot,
    diagonal,
    coupling,
    pattern,
    level,
    first_out,
    second_out,
    h_all,
    pivots,
    diagonals,
    weights,
    fields,
    sends,
    lands,
    forward,
    first_result,
    second_result,
    images,
    first_swap,
    second_swap,
    joined,
    totals,
    order,
    ranks,
    near,
    faces,
    send_sem,
    recv_sem,
    local_sem,
    rad_send,
    rad_recv,
):
    results = (first_result, second_result)
    swaps = (first_swap, second_swap)
    tiles = rhs.shape[0]
    half = rhs.shape[1] // 2
    rows = half // GROUPS
    cells = rhs.shape[2]
    columns = tiles // 2
    per_level = tiles // NLEV

    ax = lax.axis_index("ax")
    circ = lax.axis_index("circ")
    rad = lax.axis_index("rad")
    other = 1 - rad
    targets = (
        {"ax": ax - 1},
        {"ax": ax + 1},
        {"circ": lax.rem(circ + n_circ - 1, n_circ)},
        {"circ": lax.rem(circ + 1, n_circ)},
    )
    sibling = {"rad": other}

    def at_direction(d, body):
        if d == LOW_AX:
            pl.when(ax > 0)(body)
        elif d == UP_AX:
            pl.when(ax < n_ax - 1)(body)
        else:
            body()

    my_lanes = pl.ds(pl.multiple_of(rad * cells, cells), cells)
    other_lanes = pl.ds(pl.multiple_of(other * cells, cells), cells)
    my_rows = pl.ds(pl.multiple_of(rad * half, half), half)
    other_rows = pl.ds(pl.multiple_of(other * half, half), half)

    for g in range(GROUPS):
        for c in range(2):
            lands[g, c] = jnp.zeros(lands.shape[2:], BF16)

    barrier = pltpu.get_barrier_semaphore()
    for d in (LOW_C, UP_C, LOW_AX, UP_AX):

        def greet(d=d):
            pl.semaphore_signal(barrier, inc=1, device_id=targets[d], device_id_type=MESH)

        at_direction(d, greet)
    pl.semaphore_signal(barrier, inc=1, device_id=sibling, device_id_type=MESH)

    local = [
        pltpu.make_async_copy(coupling, weights.at[rad], local_sem.at[0]),
        pltpu.make_async_copy(rhs.at[:, my_rows, :], h_all.at[:, :, my_lanes], local_sem.at[1]),
        pltpu.make_async_copy(pivot, pivots.at[:, :, my_lanes], local_sem.at[2]),
        pltpu.make_async_copy(diagonal, diagonals.at[:, :, my_lanes], local_sem.at[3]),
    ]
    for copy in local:
        copy.start()

    levels = [level[t] for t in range(tiles)]
    rank = []
    for t in range(tiles):
        before = jnp.int32(0)
        for u in range(tiles):
            if u < t:
                before = before + jnp.where(levels[u] <= levels[t], 1, 0)
            elif u > t:
                before = before + jnp.where(levels[u] < levels[t], 1, 0)
        rank.append(before)
        ranks[t] = before
    for j in range(tiles):
        found = jnp.int32(0)
        for t in range(tiles):
            found = found + jnp.where(rank[t] == j, t, 0)
        order[j] = found
    upper = 2 * per_level
    slot = [
        jnp.where(
            r >= upper,
            jnp.where(r >= upper + per_level, r - upper, r - per_level),
            jnp.where(r >= per_level, r - per_level, r),
        )
        for r in rank
    ]
    for t in range(tiles):
        row, column = t // columns, t % columns
        near[4 * t] = slot[t - columns] if row == 1 else jnp.int32(6 + column // 2)
        near[4 * t + 1] = slot[t + columns] if row == 0 else jnp.int32(9 + column // 2)
        near[4 * t + 2] = slot[t - 1] if column > 0 else jnp.int32(12)
        near[4 * t + 3] = slot[t + 1] if column < columns - 1 else jnp.int32(13)
    odd = lax.rem(levels[0], 2) == 1
    for c in range(2):
        for row in range(2):
            for j in range(3):
                even_column = slot[columns * row + 2 * j]
                odd_column = slot[columns * row + 2 * j + 1]
                if (c + row) % 2 == 0:
                    faces[SLOTS * c + 3 * row + j] = jnp.where(odd, odd_column, even_column)
                else:
                    faces[SLOTS * c + 3 * row + j] = jnp.where(odd, even_column, odd_column)
        low = (slot[0], slot[columns])
        high = (slot[columns - 1], slot[2 * columns - 1])
        faces[SLOTS * c + 6] = jnp.where(odd, low[1 - c], low[c])
        faces[SLOTS * c + 7] = jnp.where(odd, high[c], high[1 - c])

    local[0].wait()

    def keep_present(t, carry):
        for d in range(4):
            block = weights[rad, t, d * cells : (d + 1) * cells, :]
            weights[rad, t, d * cells : (d + 1) * cells, :] = jnp.where(
                pattern[t, d] != 0, block, jnp.zeros_like(block)
            )
        return carry

    lax.fori_loop(0, tiles, keep_present, 0)

    inner = (ax > 0) & (ax < n_ax - 1)
    pl.when(inner)(lambda: pl.semaphore_wait(barrier, 5))
    pl.when(jnp.logical_not(inner))(lambda: pl.semaphore_wait(barrier, 4))

    def to_sibling(index, source, target):
        return pltpu.make_async_remote_copy(
            src_ref=source,
            dst_ref=target,
            send_sem=rad_send.at[index],
            recv_sem=rad_recv.at[index],
            device_id=sibling,
            device_id_type=MESH,
        )

    shares = [
        to_sibling(0, rhs.at[:, other_rows, :], h_all.at[:, :, my_lanes]),
        to_sibling(1, pivot, pivots.at[:, :, my_lanes]),
        to_sibling(2, weights.at[rad], weights.at[rad]),
        to_sibling(3, diagonal, diagonals.at[:, :, my_lanes]),
    ]
    for share in shares:
        share.start()

    def exchange(g, c, d):
        opposite = d ^ 1
        return pltpu.make_async_remote_copy(
            src_ref=sends.at[g, c, pl.ds(FIRST[d], WIDTH[d])],
            dst_ref=lands.at[g, c, pl.ds(FIRST[opposite], WIDTH[d])],
            send_sem=send_sem.at[g, c, d],
            recv_sem=recv_sem.at[g, c, opposite],
            device_id=targets[d],
            device_id_type=MESH,
        )

    def arrival(g, c, d):
        return pltpu.make_async_remote_copy(
            src_ref=sends.at[g, c, pl.ds(FIRST[d], WIDTH[d])],
            dst_ref=lands.at[g, c, pl.ds(FIRST[d], WIDTH[d])],
            send_sem=send_sem.at[g, c, d],
            recv_sem=recv_sem.at[g, c, d],
            device_id=targets[d],
            device_id_type=MESH,
        )

    def sent(g, c):
        for d in range(4):
            at_direction(d, lambda d=d: exchange(g, c, d).wait_send())

    def send(g, c, again):
        if again:
            sent(g, c)
        for d in (LOW_C, UP_C, LOW_AX, UP_AX):
            for j in range(FIRST[d], FIRST[d] + WIDTH[d]):
                sends[g, c, j] = fields[g, c, faces[SLOTS * c + j]]
            at_direction(d, lambda d=d: exchange(g, c, d).start())

    def receive(g, c):
        for d in (LOW_AX, UP_AX, LOW_C, UP_C):
            at_direction(d, lambda d=d: arrival(g, c, d).wait_recv())
        fields[g, c, 6:] = lands[g, c]

    def neighbour_sum(g, c, k, t):
        for d in range(4):
            where = near[4 * t + d]
            for r in range(2):
                joined[k, r, :, d * cells : (d + 1) * cells] = fields[
                    g, c, where, :, r * cells : (r + 1) * cells
                ]
        for r in range(2):
            totals[k, :, r * cells : (r + 1) * cells] = jnp.dot(
                joined[k, r], weights[r, t], preferred_element_type=F32
            )
        return totals[k]

    def times(values, matrices, t):
        return jnp.dot(values, matrices[t], preferred_element_type=F32)

    zero = jnp.zeros((rows, 2 * cells), BF16)

    def groups(body):
        lax.fori_loop(0, GROUPS, lambda g, carry: (body(g), carry)[1], 0)

    def group_rows(g):
        return pl.ds(pl.multiple_of(g * rows, rows), rows)

    def local_slot(lev, k):
        return (lev // 2) * per_level + k

    def forward_level(application, lev, g):
        c = lev % 2
        if lev > 0:
            receive(g, 1 - c)
        for k in range(per_level):
            j = lev * per_level + k
            t = order[j]
            if application == 0:
                term = h_all[t, group_rows(g), :].astype(F32)
                if lev > 0:
                    term = term - neighbour_sum(g, 1 - c, k, t)
            else:
                term = images[g, j] + neighbour_sum(g, 1 - c, k, t)
            solved = times(term.astype(BF16), pivots, t).astype(BF16)
            forward[g, j] = solved
            if lev == NLEV - 1:
                results[application][g, j] = solved
                fields[g, c, local_slot(lev, k)] = solved
                fields[g, c, k] = zero
            elif application == 0:
                fields[g, c, local_slot(lev, k)] = solved
                if lev < 2:
                    fields[g, c, per_level + k] = zero
            else:
                rest_part = results[0][g, j].astype(F32) - solved.astype(F32)
                fields[g, c, local_slot(lev, k)] = rest_part.astype(BF16)

    def backward_level(application, lev, g):
        c = lev % 2
        receive(g, 1 - c)
        for k in range(per_level):
            j = lev * per_level + k
            t = order[j]
            total = neighbour_sum(g, 1 - c, k, t)
            value = forward[g, j].astype(F32) - times(total.astype(BF16), pivots, t)
            value = value.astype(BF16)
            results[application][g, j] = value
            if lev > 0:
                fields[g, c, local_slot(lev, k)] = value
                if lev == 2:
                    fields[g, c, k] = zero
            elif application == 0:
                image = (times(value, diagonals, t) + total).astype(BF16)
                solved = times(image, pivots, t).astype(BF16)
                forward[g, j] = solved
                rest_part = value.astype(F32) - solved.astype(F32)
                fields[g, c, k] = rest_part.astype(BF16)

    def image_part(lev, g):
        for k in range(per_level):
            j = lev * per_level + k
            images[g, j] = times(results[0][g, j], diagonals, order[j])

    def swap(application, g):
        mine = results[application]
        out = (first_out, second_out)[application]
        for t in range(tiles):
            out[t, pl.ds(pl.multiple_of(rad * half + g * rows, rows), rows), :] = mine[
                g, ranks[t], :, my_lanes
            ]
            swaps[application][t, group_rows(g), :] = mine[g, ranks[t], :, other_lanes]

    def hand_over(application):
        out = (first_out, second_out)[application]
        return to_sibling(4 + application, swaps[application], out.at[:, my_rows, :])

    def step(body, c, again=True):
        def run(g):
            body(g)
            if c is not None:
                send(g, c, again)

        groups(run)

    for index in (1, 2):
        local[index].wait()
    shares[0].wait_recv()
    shares[1].wait_recv()
    step(lambda g: forward_level(0, 0, g), 0, False)
    local[3].wait()
    shares[2].wait_recv()
    step(lambda g: forward_level(0, 1, g), 1, False)
    shares[3].wait_recv()
    step(lambda g: forward_level(0, 2, g), 0)
    step(lambda g: forward_level(0, 3, g), 1)
    step(lambda g: backward_level(0, 2, g), 0)
    groups(lambda g: (image_part(3, g), image_part(2, g)))
    step(lambda g: backward_level(0, 1, g), 1)
    groups(lambda g: image_part(1, g))
    step(lambda g: backward_level(0, 0, g), 0)
    groups(lambda g: swap(0, g))
    hand_over(0).start()
    step(lambda g: forward_level(1, 1, g), 1)
    step(lambda g: forward_level(1, 2, g), 0)
    step(lambda g: forward_level(1, 3, g), 1)
    step(lambda g: backward_level(1, 2, g), 0)
    step(lambda g: backward_level(1, 1, g), 1)
    step(lambda g: backward_level(1, 0, g), None)
    groups(lambda g: swap(1, g))
    hand_over(1).start()
    for g in range(GROUPS):
        for c in range(2):
            sent(g, c)
    for share in shares:
        share.wait_send()
    hand_over(0).wait()
    hand_over(1).wait()


def per_device(n_ax, n_circ, adjoint_rhs, pivot_inverse, diagonal_block, coupling, pattern, wave_level):
    tiles_axial, tiles_circ, rhs_count, cells = adjoint_rhs.shape
    tiles = tiles_axial * tiles_circ
    half = rhs_count // 2
    rows = half // GROUPS
    any_space = pl.BlockSpec(memory_space=pl.ANY)
    vmem = pl.BlockSpec(memory_space=pltpu.VMEM)
    smem = pl.BlockSpec(memory_space=pltpu.SMEM)
    tile = (rows, 2 * cells)
    out = jax.ShapeDtypeStruct((tiles, rhs_count, cells), BF16)
    first, second = pl.pallas_call(
        functools.partial(kernel, n_ax, n_circ),
        out_shape=(out, out),
        in_specs=[any_space] * 4 + [smem] * 2,
        out_specs=(vmem, vmem),
        scratch_shapes=[
            pltpu.VMEM((tiles, half, 2 * cells), BF16),
            pltpu.VMEM((tiles, 2 * cells, 2 * cells), BF16),
            pltpu.VMEM((tiles, 2 * cells, 2 * cells), BF16),
            pltpu.VMEM((2, tiles, 4 * cells, cells), BF16),
            pltpu.VMEM((GROUPS, 2, 6 + SLOTS, *tile), BF16),
            pltpu.VMEM((GROUPS, 2, SLOTS, *tile), BF16),
            pltpu.VMEM((GROUPS, 2, SLOTS, *tile), BF16),
            pltpu.VMEM((GROUPS, tiles, *tile), BF16),
            pltpu.VMEM((GROUPS, tiles, *tile), BF16),
            pltpu.VMEM((GROUPS, tiles, *tile), BF16),
            pltpu.VMEM((GROUPS, tiles, *tile), F32),
            pltpu.VMEM((tiles, half, cells), BF16),
            pltpu.VMEM((tiles, half, cells), BF16),
            pltpu.VMEM((tiles // NLEV, 2, rows, 4 * cells), BF16),
            pltpu.VMEM((tiles // NLEV, rows, 2 * cells), F32),
            pltpu.SMEM((tiles,), jnp.int32),
            pltpu.SMEM((tiles,), jnp.int32),
            pltpu.SMEM((4 * tiles,), jnp.int32),
            pltpu.SMEM((2 * SLOTS,), jnp.int32),
            pltpu.SemaphoreType.DMA((GROUPS, 2, 4)),
            pltpu.SemaphoreType.DMA((GROUPS, 2, 4)),
            pltpu.SemaphoreType.DMA((4,)),
            pltpu.SemaphoreType.DMA((6,)),
            pltpu.SemaphoreType.DMA((6,)),
        ],
        compiler_params=pltpu.CompilerParams(
            collective_id=0, has_side_effects=True, vmem_limit_bytes=40 << 20
        ),
    )(
        adjoint_rhs.reshape(tiles, rhs_count, cells),
        pivot_inverse.reshape(tiles, 2 * cells, cells),
        diagonal_block.reshape(tiles, 2 * cells, cells),
        coupling.reshape(tiles, 4 * cells, cells),
        pattern.reshape(tiles, 4),
        wave_level.reshape(tiles),
    )
    shape = (tiles_axial, tiles_circ, rhs_count, cells)
    return first.reshape(shape), second.reshape(shape)


def solution(mesh):
    return jax.shard_map(
        functools.partial(per_device, mesh.shape["ax"], mesh.shape["circ"]),
        mesh=mesh,
        in_specs=(
            P("ax", "circ", None, "rad"),
            P("ax", "circ", None, "rad"),
            P("ax", "circ", None, "rad"),
            P("ax", "circ", "rad", None, None, None),
            P("ax", "circ", "rad", None),
            P("ax", "circ"),
        ),
        out_specs=(P("ax", "circ", None, "rad"), P("ax", "circ", None, "rad")),
        check_vma=False,
    )
```

time: 588 us -> 151 us (0.26)
  the two profiles are of different devices: /device:TPU:31 before, /device:TPU:17 now
where the time goes in v2:
time: 151 us; the launch traced here: 150 us
  Pallas kernels  142 us (94%)
  local copies, waits for them, and re-layouts  7.79 us (5%)
    pallas_call x1, Pallas kernels, per_device(): pl.pallas_call(functools.partial(kernel, n_ax, n_circ), out_shape=(out, o...  142 us
    unnamed x11, local copies, waits for them, and re-layouts  6.85 us

profile of v2, /device:TPU:17, one launch (start us, length us, event | category | flops | bytes accessed | tf_op | source)
XLA Modules:
  0.0 150.4 jit_solution(16554553525792573328)
XLA Ops:
  0.6 0.8 reshape.33.level
  1.4 0.7 copy.8
  2.1 0.1 reshape.32
  2.2 0.1 copy.9.pattern
  2.3 0.0 copy-start
  2.3 1.4 copy-done
  3.7 0.0 copy-start.1
  3.7 1.1 copy-done.1
  4.8 0.0 copy-start.2
  4.8 1.1 copy-done.2
  5.9 0.0 copy-start.3
  5.9 1.0 copy-done.3
  6.9 142.0 %shard_map.77 = (bf16[12,128,128]{2,1,0:T(8,128)(2,1)S(1)}, bf16[12,128,128]{2,1,0:T(8,128)(2,1)S(1)}) custom-call(bf16[12,128,128]{2,1,0:T(8,128)(2,1)S(1)} %bitcast.13, bf16[12,256,128]{2,1,0:T(8,128)(2,1)S(1)} %bitcast.9, bf16[12,256,128]{2,1,0:T(8,128)(2,1)S(1)} %bitcast.10, bf16[12,512,128]{2,1,0:T(8,128)(2,1)S(1)} %bitcast.8, ...), custom_call_target="tpu_custom_call" | custom-call | tf_op jit(solution)/shard_map/pallas_call | solution.py:378
  149.0 0.7 copy.12
  149.7 0.7 copy.13
Async XLA Ops:
  2.3 1.4 copy-start
  3.7 1.1 copy-start.1
  4.8 1.1 copy-start.2
  5.9 1.0 copy-start.3

commit v3 on v2

--- a/solution.py
+++ b/solution.py
@@ -10,8 +10,9 @@
 MESH = pl.DeviceIdType.MESH
 F32 = jnp.float32
 BF16 = jnp.bfloat16
-GROUPS = 2
+GROUPS = 4
 NLEV = 4
+PARTS = 2
 LOW_AX, UP_AX, LOW_C, UP_C = range(4)
 FIRST = (0, 3, 6, 7)
 WIDTH = (3, 3, 1, 1)
@@ -33,6 +34,7 @@
     pivots,
     diagonals,
     weights,
+    own_weights,
     fields,
     sends,
     lands,
@@ -42,6 +44,8 @@
     images,
     first_swap,
     second_swap,
+    first_kept,
+    second_kept,
     joined,
     totals,
     order,
@@ -56,6 +60,7 @@
 ):
     results = (first_result, second_result)
     swaps = (first_swap, second_swap)
+    kept = (first_kept, second_kept)
     tiles = rhs.shape[0]
     half = rhs.shape[1] // 2
     rows = half // GROUPS
@@ -102,7 +107,7 @@
     pl.semaphore_signal(barrier, inc=1, device_id=sibling, device_id_type=MESH)
 
     local = [
-        pltpu.make_async_copy(coupling, weights.at[rad], local_sem.at[0]),
+        pltpu.make_async_copy(coupling, own_weights, local_sem.at[0]),
         pltpu.make_async_copy(rhs.at[:, my_rows, :], h_all.at[:, :, my_lanes], local_sem.at[1]),
         pltpu.make_async_copy(pivot, pivots.at[:, :, my_lanes], local_sem.at[2]),
         pltpu.make_async_copy(diagonal, diagonals.at[:, :, my_lanes], local_sem.at[3]),
@@ -110,7 +115,7 @@
     for copy in local:
         copy.start()
 
-    levels = [level[t] for t in range(tiles)]
+    levels = [level[t // columns, t % columns] for t in range(tiles)]
     rank = []
     for t in range(tiles):
         before = jnp.int32(0)
@@ -160,13 +165,15 @@
 
     def keep_present(t, carry):
         for d in range(4):
-            block = weights[rad, t, d * cells : (d + 1) * cells, :]
-            weights[rad, t, d * cells : (d + 1) * cells, :] = jnp.where(
-                pattern[t, d] != 0, block, jnp.zeros_like(block)
+            block = own_weights[t, d * cells : (d + 1) * cells, :]
+            own_weights[t, d * cells : (d + 1) * cells, :] = jnp.where(
+                pattern[t // columns, 0, d, lax.rem(t, columns)] != 0, block, jnp.zeros_like(block)
             )
         return carry
 
     lax.fori_loop(0, tiles, keep_present, 0)
+    local.append(pltpu.make_async_copy(own_weights, weights.at[:, :, my_lanes], local_sem.at[4]))
+    local[4].start()
 
     inner = (ax > 0) & (ax < n_ax - 1)
     pl.when(inner)(lambda: pl.semaphore_wait(barrier, 5))
@@ -185,7 +192,7 @@
     shares = [
         to_sibling(0, rhs.at[:, other_rows, :], h_all.at[:, :, my_lanes]),
         to_sibling(1, pivot, pivots.at[:, :, my_lanes]),
-        to_sibling(2, weights.at[rad], weights.at[rad]),
+        to_sibling(2, own_weights, weights.at[:, :, my_lanes]),
         to_sibling(3, diagonal, diagonals.at[:, :, my_lanes]),
     ]
     for share in shares:
@@ -233,13 +240,14 @@
         for d in range(4):
             where = near[4 * t + d]
             for r in range(2):
-                joined[k, r, :, d * cells : (d + 1) * cells] = fields[
+                joined[k, r * rows : (r + 1) * rows, d * cells : (d + 1) * cells] = fields[
                     g, c, where, :, r * cells : (r + 1) * cells
                 ]
+        both = jnp.dot(joined[k], weights[t], preferred_element_type=F32)
         for r in range(2):
-            totals[k, :, r * cells : (r + 1) * cells] = jnp.dot(
-                joined[k, r], weights[r, t], preferred_element_type=F32
-            )
+            totals[k, :, r * cells : (r + 1) * cells] = both[
+                r * rows : (r + 1) * rows, r * cells : (r + 1) * cells
+            ]
         return totals[k]
 
     def times(values, matrices, t):
@@ -311,16 +319,27 @@
 
     def swap(application, g):
         mine = results[application]
-        out = (first_out, second_out)[application]
         for t in range(tiles):
-            out[t, pl.ds(pl.multiple_of(rad * half + g * rows, rows), rows), :] = mine[
-                g, ranks[t], :, my_lanes
-            ]
+            kept[application][t, group_rows(g), :] = mine[g, ranks[t], :, my_lanes]
             swaps[application][t, group_rows(g), :] = mine[g, ranks[t], :, other_lanes]
 
-    def hand_over(application):
-        out = (first_out, second_out)[application]
-        return to_sibling(4 + application, swaps[application], out.at[:, my_rows, :])
+    def hand_over(g):
+        group_of_all = pl.ds(pl.multiple_of(rad * half + g * rows, rows), rows)
+        return (
+            to_sibling(
+                5 + g, second_swap.at[:, group_rows(g), :], second_out.at[:, group_of_all, :]
+            ),
+            pltpu.make_async_copy(
+                second_kept.at[:, group_rows(g), :],
+                second_out.at[:, group_of_all, :],
+                local_sem.at[6 + g],
+            ),
+        )
+
+    first_hand_over = (
+        to_sibling(4, first_swap, first_out.at[:, my_rows, :]),
+        pltpu.make_async_copy(first_kept, first_out.at[:, my_rows, :], local_sem.at[5]),
+    )
 
     def step(body, c, again=True):
         def run(g):
@@ -336,6 +355,7 @@
     shares[1].wait_recv()
     step(lambda g: forward_level(0, 0, g), 0, False)
     local[3].wait()
+    local[4].wait()
     shares[2].wait_recv()
     step(lambda g: forward_level(0, 1, g), 1, False)
     shares[3].wait_recv()
@@ -347,22 +367,36 @@
     groups(lambda g: image_part(1, g))
     step(lambda g: backward_level(0, 0, g), 0)
     groups(lambda g: swap(0, g))
-    hand_over(0).start()
+    for copy in first_hand_over:
+        copy.start()
     step(lambda g: forward_level(1, 1, g), 1)
     step(lambda g: forward_level(1, 2, g), 0)
     step(lambda g: forward_level(1, 3, g), 1)
     step(lambda g: backward_level(1, 2, g), 0)
     step(lambda g: backward_level(1, 1, g), 1)
-    step(lambda g: backward_level(1, 0, g), None)
-    groups(lambda g: swap(1, g))
-    hand_over(1).start()
+
+    def finish(g):
+        backward_level(1, 0, g)
+        swap(1, g)
+        for copy in hand_over(g):
+            copy.start()
+
+    groups(finish)
     for g in range(GROUPS):
         for c in range(2):
             sent(g, c)
     for share in shares:
         share.wait_send()
-    hand_over(0).wait()
-    hand_over(1).wait()
+    for copy in first_hand_over:
+        copy.wait()
+    for g in range(GROUPS):
+        for copy in hand_over(g):
+            copy.wait()
+
+
+def write_out(first, second, first_out, second_out):
+    first_out[...] = first[...]
+    second_out[...] = second[...]
 
 
 def per_device(n_ax, n_circ, adjoint_rhs, pivot_inverse, diagonal_block, coupling, pattern, wave_level):
@@ -370,21 +404,21 @@
     tiles = tiles_axial * tiles_circ
     half = rhs_count // 2
     rows = half // GROUPS
-    any_space = pl.BlockSpec(memory_space=pl.ANY)
-    vmem = pl.BlockSpec(memory_space=pltpu.VMEM)
+    hbm = pl.BlockSpec(memory_space=pl.ANY)
     smem = pl.BlockSpec(memory_space=pltpu.SMEM)
     tile = (rows, 2 * cells)
     out = jax.ShapeDtypeStruct((tiles, rhs_count, cells), BF16)
     first, second = pl.pallas_call(
         functools.partial(kernel, n_ax, n_circ),
         out_shape=(out, out),
-        in_specs=[any_space] * 4 + [smem] * 2,
-        out_specs=(vmem, vmem),
+        in_specs=[hbm] * 4 + [smem] * 2,
+        out_specs=(hbm, hbm),
         scratch_shapes=[
             pltpu.VMEM((tiles, half, 2 * cells), BF16),
             pltpu.VMEM((tiles, 2 * cells, 2 * cells), BF16),
             pltpu.VMEM((tiles, 2 * cells, 2 * cells), BF16),
-            pltpu.VMEM((2, tiles, 4 * cells, cells), BF16),
+            pltpu.VMEM((tiles, 4 * cells, 2 * cells), BF16),
+            pltpu.VMEM((tiles, 4 * cells, cells), BF16),
             pltpu.VMEM((GROUPS, 2, 6 + SLOTS, *tile), BF16),
             pltpu.VMEM((GROUPS, 2, SLOTS, *tile), BF16),
             pltpu.VMEM((GROUPS, 2, SLOTS, *tile), BF16),
@@ -394,7 +428,9 @@
             pltpu.VMEM((GROUPS, tiles, *tile), F32),
             pltpu.VMEM((tiles, half, cells), BF16),
             pltpu.VMEM((tiles, half, cells), BF16),
-            pltpu.VMEM((tiles // NLEV, 2, rows, 4 * cells), BF16),
+            pltpu.VMEM((tiles, half, cells), BF16),
+            pltpu.VMEM((tiles, half, cells), BF16),
+            pltpu.VMEM((tiles // NLEV, 2 * rows, 4 * cells), BF16),
             pltpu.VMEM((tiles // NLEV, rows, 2 * cells), F32),
             pltpu.SMEM((tiles,), jnp.int32),
             pltpu.SMEM((tiles,), jnp.int32),
@@ -402,21 +438,29 @@
             pltpu.SMEM((2 * SLOTS,), jnp.int32),
             pltpu.SemaphoreType.DMA((GROUPS, 2, 4)),
             pltpu.SemaphoreType.DMA((GROUPS, 2, 4)),
-            pltpu.SemaphoreType.DMA((4,)),
-            pltpu.SemaphoreType.DMA((6,)),
-            pltpu.SemaphoreType.DMA((6,)),
+            pltpu.SemaphoreType.DMA((6 + GROUPS,)),
+            pltpu.SemaphoreType.DMA((5 + GROUPS,)),
+            pltpu.SemaphoreType.DMA((5 + GROUPS,)),
         ],
         compiler_params=pltpu.CompilerParams(
-            collective_id=0, has_side_effects=True, vmem_limit_bytes=40 << 20
+            collective_id=0, has_side_effects=True, vmem_limit_bytes=60 << 20
         ),
     )(
         adjoint_rhs.reshape(tiles, rhs_count, cells),
         pivot_inverse.reshape(tiles, 2 * cells, cells),
         diagonal_block.reshape(tiles, 2 * cells, cells),
         coupling.reshape(tiles, 4 * cells, cells),
-        pattern.reshape(tiles, 4),
-        wave_level.reshape(tiles),
+        jnp.transpose(pattern, (0, 2, 3, 1)),
+        wave_level,
     )
+    part = pl.BlockSpec((tiles // PARTS, rhs_count, cells), lambda i: (i, 0, 0))
+    first, second = pl.pallas_call(
+        write_out,
+        out_shape=(out, out),
+        grid=(PARTS,),
+        in_specs=[part] * 2,
+        out_specs=(part, part),
+    )(first, second)
     shape = (tiles_axial, tiles_circ, rhs_count, cells)
     return first.reshape(shape), second.reshape(shape)
 

time: 151 us -> 141 us (0.934)
  local copies, waits for them, and re-layouts: 7.79 us -> 0 us
  Pallas kernels: 142 us -> 140 us
    unnamed x11 -> x0, local copies, waits for them, and re-layouts: 6.85 us -> none
    pallas_call x1, Pallas kernels: 142 us -> 138 us  [per_device(): pl.pallas_call(functools.partial(kernel, n_ax, n_circ), out_shape=(out, o...]
    pallas_call x0 -> x1, Pallas kernels: none -> 2 us  [per_device(): pl.pallas_call(write_out, out_shape=(out, out), grid=(PARTS,), in_specs=[...]
where the time goes in v3:
time: 141 us
  Pallas kernels  140 us (99%)
    pallas_call x1, Pallas kernels, per_device(): pl.pallas_call(functools.partial(kernel, n_ax, n_circ), out_shape=(out, o...  138 us

profile of v3, /device:TPU:17, one launch (start us, length us, event | category | flops | bytes accessed | tf_op | source)
XLA Modules:
  0.0 141.0 jit_solution(10197039090117640424)
XLA Ops:
  0.6 138.4 %shard_map.77 = (bf16[12,128,128]{2,1,0:T(8,128)(2,1)}, bf16[12,128,128]{2,1,0:T(8,128)(2,1)}) custom-call(bf16[12,128,128]{2,1,0:T(8,128)(2,1)} %bitcast.10, bf16[12,256,128]{2,1,0:T(8,128)(2,1)} %bitcast.8, bf16[12,256,128]{2,1,0:T(8,128)(2,1)} %bitcast.9, bf16[12,512,128]{2,1,0:T(8,128)(2,1)} %bitcast.7, s32[2,1,4,6]{3,2,1,0:T(4,128)} %bitcast.11, ...), custom_call_target="tpu_custom_call" | custom-call | tf_op jit(solution)/shard_map/pallas_call | solution.py:411
  139.0 2.0 %shard_map.78 = (bf16[12,128,128]{2,1,0:T(8,128)(2,1)}, bf16[12,128,128]{2,1,0:T(8,128)(2,1)}) custom-call(bf16[12,128,128]{2,1,0:T(8,128)(2,1)} %get-tuple-element.6.first, bf16[12,128,128]{2,1,0:T(8,128)(2,1)} %get-tuple-element.7.second), custom_call_target="tpu_custom_call" | custom-call | tf_op jit(solution)/shard_map/pallas_call | solution.py:457

commit v4 on v3

--- a/solution.py
+++ b/solution.py
@@ -236,19 +236,24 @@
             at_direction(d, lambda d=d: arrival(g, c, d).wait_recv())
         fields[g, c, 6:] = lands[g, c]
 
-    def neighbour_sum(g, c, k, t):
-        for d in range(4):
-            where = near[4 * t + d]
+    def neighbour_sums(g, c, chosen):
+        beside = [[fields[g, c, near[4 * t + d]] for d in range(4)] for t in chosen]
+        for k in range(per_level):
+            for d in range(4):
+                for r in range(2):
+                    joined[k, r * rows : (r + 1) * rows, d * cells : (d + 1) * cells] = beside[k][
+                        d
+                    ][:, r * cells : (r + 1) * cells]
+        both = [
+            jnp.dot(joined[k], weights[t], preferred_element_type=F32)
+            for k, t in enumerate(chosen)
+        ]
+        for k in range(per_level):
             for r in range(2):
-                joined[k, r * rows : (r + 1) * rows, d * cells : (d + 1) * cells] = fields[
-                    g, c, where, :, r * cells : (r + 1) * cells
+                totals[k, :, r * cells : (r + 1) * cells] = both[k][
+                    r * rows : (r + 1) * rows, r * cells : (r + 1) * cells
                 ]
-        both = jnp.dot(joined[k], weights[t], preferred_element_type=F32)
-        for r in range(2):
-            totals[k, :, r * cells : (r + 1) * cells] = both[
-                r * rows : (r + 1) * rows, r * cells : (r + 1) * cells
-            ]
-        return totals[k]
+        return [totals[k] for k in range(per_level)]
 
     def times(values, matrices, t):
         return jnp.dot(values, matrices[t], preferred_element_type=F32)
@@ -266,50 +271,64 @@
 
     def forward_level(application, lev, g):
         c = lev % 2
+        places = [lev * per_level + k for k in range(per_level)]
+        chosen = [order[j] for j in places]
+        if application == 0:
+            terms = [h_all[t, group_rows(g), :].astype(F32) for t in chosen]
+        else:
+            terms = [images[g, j] for j in places]
         if lev > 0:
             receive(g, 1 - c)
-        for k in range(per_level):
-            j = lev * per_level + k
-            t = order[j]
+            sums = neighbour_sums(g, 1 - c, chosen)
             if application == 0:
-                term = h_all[t, group_rows(g), :].astype(F32)
-                if lev > 0:
-                    term = term - neighbour_sum(g, 1 - c, k, t)
+                terms = [term - total for term, total in zip(terms, sums)]
             else:
-                term = images[g, j] + neighbour_sum(g, 1 - c, k, t)
-            solved = times(term.astype(BF16), pivots, t).astype(BF16)
-            forward[g, j] = solved
+                terms = [term + total for term, total in zip(terms, sums)]
+        solved = [
+            times(term.astype(BF16), pivots, t).astype(BF16) for term, t in zip(terms, chosen)
+        ]
+        if application == 1 and lev < NLEV - 1:
+            firsts = [results[0][g, j].astype(F32) for j in places]
+        for k, j in enumerate(places):
+            forward[g, j] = solved[k]
             if lev == NLEV - 1:
-                results[application][g, j] = solved
-                fields[g, c, local_slot(lev, k)] = solved
+                results[application][g, j] = solved[k]
+                fields[g, c, local_slot(lev, k)] = solved[k]
                 fields[g, c, k] = zero
             elif application == 0:
-                fields[g, c, local_slot(lev, k)] = solved
+                fields[g, c, local_slot(lev, k)] = solved[k]
                 if lev < 2:
                     fields[g, c, per_level + k] = zero
             else:
-                rest_part = results[0][g, j].astype(F32) - solved.astype(F32)
+                rest_part = firsts[k] - solved[k].astype(F32)
                 fields[g, c, local_slot(lev, k)] = rest_part.astype(BF16)
 
     def backward_level(application, lev, g):
         c = lev % 2
+        places = [lev * per_level + k for k in range(per_level)]
+        chosen = [order[j] for j in places]
+        forwards = [forward[g, j].astype(F32) for j in places]
         receive(g, 1 - c)
-        for k in range(per_level):
-            j = lev * per_level + k
-            t = order[j]
-            total = neighbour_sum(g, 1 - c, k, t)
-            value = forward[g, j].astype(F32) - times(total.astype(BF16), pivots, t)
-            value = value.astype(BF16)
-            results[application][g, j] = value
+        sums = neighbour_sums(g, 1 - c, chosen)
+        values = [
+            (forwards[k] - times(sums[k].astype(BF16), pivots, t)).astype(BF16)
+            for k, t in enumerate(chosen)
+        ]
+        if lev == 0 and application == 0:
+            pictures = [
+                (times(values[k], diagonals, t) + sums[k]).astype(BF16)
+                for k, t in enumerate(chosen)
+            ]
+            solved = [times(pictures[k], pivots, t).astype(BF16) for k, t in enumerate(chosen)]
+        for k, j in enumerate(places):
+            results[application][g, j] = values[k]
             if lev > 0:
-                fields[g, c, local_slot(lev, k)] = value
+                fields[g, c, local_slot(lev, k)] = values[k]
                 if lev == 2:
                     fields[g, c, k] = zero
             elif application == 0:
-                image = (times(value, diagonals, t) + total).astype(BF16)
-                solved = times(image, pivots, t).astype(BF16)
-                forward[g, j] = solved
-                rest_part = value.astype(F32) - solved.astype(F32)
+                forward[g, j] = solved[k]
+                rest_part = values[k].astype(F32) - solved[k].astype(F32)
                 fields[g, c, k] = rest_part.astype(BF16)
 
     def image_part(lev, g):

time: 141 us -> 136 us (0.965)
  the two profiles are of different devices: /device:TPU:17 before, /device:TPU:49 now
where the time goes in v4:
time: 136 us
  Pallas kernels  136 us (100%)
    pallas_call x1, Pallas kernels, per_device(): pl.pallas_call(functools.partial(kernel, n_ax, n_circ), out_shape=(out, o...  134 us

profile of v4, /device:TPU:49, one launch (start us, length us, event | category | flops | bytes accessed | tf_op | source)
XLA Modules:
  0.0 136.3 jit_solution(11153771529315672517)
XLA Ops:
  0.6 133.6 %shard_map.77 = (bf16[12,128,128]{2,1,0:T(8,128)(2,1)}, bf16[12,128,128]{2,1,0:T(8,128)(2,1)}) custom-call(bf16[12,128,128]{2,1,0:T(8,128)(2,1)} %bitcast.10, bf16[12,256,128]{2,1,0:T(8,128)(2,1)} %bitcast.8, bf16[12,256,128]{2,1,0:T(8,128)(2,1)} %bitcast.9, bf16[12,512,128]{2,1,0:T(8,128)(2,1)} %bitcast.7, s32[2,1,4,6]{3,2,1,0:T(4,128)} %bitcast.11, ...), custom_call_target="tpu_custom_call" | custom-call | tf_op jit(solution)/shard_map/pallas_call | solution.py:430
  134.3 2.0 %shard_map.78 = (bf16[12,128,128]{2,1,0:T(8,128)(2,1)}, bf16[12,128,128]{2,1,0:T(8,128)(2,1)}) custom-call(bf16[12,128,128]{2,1,0:T(8,128)(2,1)} %get-tuple-element.6.first, bf16[12,128,128]{2,1,0:T(8,128)(2,1)} %get-tuple-element.7.second), custom_call_target="tpu_custom_call" | custom-call | tf_op jit(solution)/shard_map/pallas_call | solution.py:476
